TPU v7x, 128 devices: a whole 4x4x4 slice. The times are simulated.
128 devices in a mesh: wide: 32 (over y, z, core), node: 4 (over x).
Axes of the slice: x: 4, y: 4, z: 4, core: 2. Of those that a mesh axis runs over, the one named last changes fastest.
Arguments:
- item_factors: float32 [262144, 256], P('wide', 'node')
- need_owner: int32 [1024, 1], P('wide'), may hold values from 0 to 31; in each aligned block of 32 rows (0 to 31, 32 to 63, ...) at most 2 rows name the same one
- need_slot: int32 [1024], P('wide'), may hold values from 0 to 63
- block_index: int32 [8192], P(('wide', 'node')), may hold values from 0 to 63, as said below
- block_count: int32 [128], P(('wide', 'node')), may hold values from 16 to 64
- weights: float32 [8192, 128, 128], P(('wide', 'node')), may hold values from 1 to 40
- user_old: float32 [32768, 256], P(('wide', 'node')), may hold values from -2 to 2
Outputs:
- users_new: float32 [32768, 256], P(('wide', 'node'))
- user_gram: float32 [256, 256], replicated
- at_owners: float32 [32, 32, 1024, 256], P('wide', None, 'node')
Inputs may be any that keep to these rules, and one draw needn't show every extreme that they name: `need_owner`: within the 32 entries of one group, no item group is named by more than 2 entries. `block_index`: the 64 entries of one device are all different.
All inputs are finite; a program needn't handle non-finite values.
Results may differ from a plain program's by a relative error of at most 0.0003.
Values sent between devices are 32-bit elements; how exact they have to be, the bound alone decides.
A program may use at most 128 MiB of HBM per device.

v0:
```python
import jax
import jax.numpy as jnp
from jax import lax
from jax.sharding import PartitionSpec as P

TILE = 128
ITERS = 2
NEED = 32


highest = lax.Precision.HIGHEST
ridge = 1.0
tiny_eps = 1e-06


def operate(direction, item_gram, picked_tiles, live_weights, tile_of_block, block_hot):
    picked = direction[tile_of_block]
    scores = jnp.einsum("btk,bik->bti", picked, picked_tiles, precision=highest)
    spread = jnp.einsum("bti,bik->btk", scores * live_weights, picked_tiles, precision=highest)
    local_term = jnp.einsum("bu,btk->utk", block_hot, spread, precision=highest)
    flat_rows = direction.reshape(-1, direction.shape[2])
    global_part = jnp.dot(flat_rows, item_gram, precision=highest) + ridge * flat_rows
    return global_part.reshape(direction.shape) + local_term


def solve_users(user_block, list_tiles, block_weights, index_list, count, item_gram):
    tiles_per_user = user_block.shape[0] // TILE
    rank_width = user_block.shape[1]
    tile_of_block = index_list // NEED
    list_position = index_list % NEED
    picked_tiles = list_tiles[list_position]
    live_mask = (jnp.arange(index_list.shape[0], dtype=jnp.int32) < count).astype(jnp.float32)
    live_weights = block_weights * live_mask[:, None, None]
    block_hot = (
        tile_of_block[:, None] == jnp.arange(tiles_per_user, dtype=jnp.int32)[None, :]
    ).astype(jnp.float32)
    pulled = jnp.einsum(
        "bti,bik->btk", live_weights + live_mask[:, None, None], picked_tiles, precision=highest
    )
    target = jnp.einsum("bu,btk->utk", block_hot, pulled, precision=highest)
    current = user_block.reshape(tiles_per_user, TILE, rank_width)
    residual = target - operate(
        current, item_gram, picked_tiles, live_weights, tile_of_block, block_hot
    )
    direction = residual
    norm_sq = jnp.sum(residual * residual, axis=2, keepdims=True)
    for iteration in range(ITERS):
        applied = operate(
            direction, item_gram, picked_tiles, live_weights, tile_of_block, block_hot
        )
        curvature = jnp.sum(direction * applied, axis=2, keepdims=True)
        step_size = norm_sq / (curvature + tiny_eps)
        current = current + step_size * direction
        residual = residual - step_size * applied
        norm_next = jnp.sum(residual * residual, axis=2, keepdims=True)
        direction = residual + norm_next / (norm_sq + tiny_eps) * direction
        norm_sq = norm_next
    return current.reshape(-1, rank_width)


def body(item_factors, need_owner, need_slot, block_index, block_count, weights, user_old):
    wide_count = lax.axis_size("wide")
    node_count = lax.axis_size("node")
    quarter = item_factors.shape[1]
    rank_width = quarter * node_count
    capacity = 2 * NEED // wide_count
    full_rows = lax.all_to_all(item_factors, "node", split_axis=0, concat_axis=1, tiled=True)
    partial_gram = jnp.dot(full_rows.T, full_rows, precision=highest)
    item_gram = lax.psum(partial_gram, ("wide", "node"))
    owner_of = need_owner[:, 0]
    position = jnp.arange(NEED, dtype=jnp.int32)
    same_owner = owner_of[:, None] == owner_of[None, :]
    rank_in = jnp.sum(
        (same_owner & (position[None, :] < position[:, None])).astype(jnp.int32), axis=1
    )
    slot_place = owner_of * capacity + rank_in
    one_hot = (
        slot_place[:, None] == jnp.arange(wide_count * capacity, dtype=jnp.int32)[None, :]
    ).astype(jnp.int32)
    request = jnp.sum(one_hot * need_slot[:, None], axis=0).reshape(wide_count, capacity)
    local_tiles = item_factors.reshape(-1, TILE, quarter)
    outgoing = jnp.repeat(request, node_count, axis=0)
    asked = lax.all_to_all(outgoing, ("wide", "node"), split_axis=0, concat_axis=0, tiled=True)
    served = local_tiles[asked]
    arrived = lax.all_to_all(served, ("wide", "node"), split_axis=0, concat_axis=0, tiled=True)
    arrived = arrived.reshape(wide_count, node_count, capacity, TILE, quarter)
    full_tiles = arrived.transpose(0, 2, 3, 1, 4).reshape(wide_count * capacity, TILE, rank_width)
    list_tiles = full_tiles[slot_place]
    users_new = solve_users(user_old, list_tiles, weights, block_index, block_count[0], item_gram)
    partial_users = jnp.dot(users_new.T, users_new, precision=highest)
    user_gram = lax.psum(partial_users, ("wide", "node"))
    named_owner = jnp.any(
        owner_of[:, None] == jnp.arange(wide_count, dtype=jnp.int32)[None, :], axis=0
    ).astype(jnp.float32)
    outgoing_users = named_owner[:, None, None] * users_new[None]
    received = lax.all_to_all(outgoing_users, "wide", split_axis=0, concat_axis=0, tiled=True)
    return (users_new, user_gram, received[None])


def solution(mesh):
    placed = (
        P("wide", "node"),
        P("wide", None),
        P("wide"),
        P(("wide", "node")),
        P(("wide", "node")),
        P(("wide", "node"), None, None),
        P(("wide", "node"), None),
    )
    return jax.shard_map(
        body,
        mesh=mesh,
        in_specs=placed,
        out_specs=(P(("wide", "node"), None), P(), P("wide", None, "node", None)),
        check_vma=False,
    )
```

profile of v0, /device:TPU:1, one launch (start us, length us, event | category | flops | bytes accessed | tf_op | source)
XLA Modules:
  0.0 704.6 jit_solution(10535034858438535031)
XLA Ops:
  10.2 11.5 %all-to-all-start = ((s32[128,1,2]{2,1,0:T(1,128)}), s32[128,1,2]{2,1,0:T(1,128)S(1)}, u32[]{:S(2)}, u32[]{:S(2)}) async-start(s32[128,1,2]{2,1,0:T(1,128)} %bitcast.6), calls=%async_computation | async-start | bytes 131072 | tf_op jit(solution)/shard_map/all_to_all | solution.py:83
  21.7 3.1 copy.153
  24.9 6.7 all-to-all-done
  31.6 4.4 all-to-all-start.2
  36.0 1.9 copy_bitcast_fusion.1
  38.0 4.5 gather_fusion
  42.6 19.6 %all-to-all-done.2 = f32[4,2048,64]{1,2,0:T(8,128)} async-done(((f32[4,2048,64]{1,2,0:T(8,128)}), f32[4,2048,64]{1,2,0:T(8,128)}, u32[]{:S(2)}, u32[]{:S(2)}) %all-to-all-start.2) | async-done | bytes 2097184 | tf_op jit(solution)/shard_map/all_to_all | solution.py:67
  62.1 6.0 all-to-all-start.1
  69.2 4.8 fusion.39
  74.1 4.3 gather_fusion.3
  78.4 204.9 %all-reduce.3.cloned.1.call-done = f32[256,256]{1,0:T(8,128)} async-done(((f32[256,256]{1,0:T(8,128)}), f32[256,256]{1,0:T(8,128)}) %all-reduce.3.cloned.1.call-update) | async-done | bytes 262160 | tf_op jit(solution)/shard_map/psum | solution.py:69
  284.7 8.4 %copy.99 = f32[32,2,128,4,64]{2,4,3,1,0:T(8,128)} copy(f32[32,2,128,4,64]{2,4,1,3,0:T(8,128)} %bitcast.10) | data formatting | bytes 16777216 | tf_op jit(solution)/shard_map/transpose | solution.py:87
  293.1 6.2 gather_fusion.1
  299.3 6.7 gather_fusion.2
  305.9 16.8 %fusion.40 = f32[64,128,128]{2,1,0:T(8,128)} fusion(f32[64,128,256]{2,1,0:T(8,128)} %gather_fusion.3, f32[64,128,256]{1,2,0:T(8,128)} %gather_fusion.2), kind=kOutput, calls=%fused_computation.87 | convolution fusion | flops 3221225472 | bytes 20971520 | tf_op jit(solution)/shard_map/btk,bik->bti/dot_general | solution.py:18
  322.7 11.5 %fusion.14 = f32[64,128,256]{2,1,0:T(8,128)} fusion(f32[64,128,256]{1,2,0:T(8,128)S(1)} %copy-done, f32[64,128,128]{2,1,0:T(8,128)} %param.12, f32[64]{0:T(128)S(1)} %compare_convert_fusion), kind=kOutput, calls=%fused_computation.21 | convolution fusion | flops 3223322624 | bytes 20971776 | tf_op jit(solution)/shard_map/bti,bik->btk/dot_general | solution.py:37
  334.2 12.3 %fusion.12 = f32[64,128,256]{2,1,0:T(8,128)} fusion(f32[64,128,256]{1,2,0:T(8,128)S(1)} %copy-done, f32[64,128,128]{2,1,0:T(8,128)} %fusion.40, f32[64,128,128]{2,1,0:T(8,128)} %param.12, f32[64]{0:T(128)S(1)} %compare_convert_fusion), kind=kOutput, calls=%fused_computation.19 | convolution fusion | flops 3223322624 | bytes 25166080 | tf_op jit(solution)/shard_map/bti,bik->btk/dot_general | solution.py:19
  346.4 10.6 %fusion.4 = f32[2,128,256]{2,0,1:T(2,128)S(1)} fusion(f32[64,128,256]{2,1,0:T(8,128)} %fusion.12, s32[64]{0:T(128)S(1)} %get-tuple-element.6), kind=kOutput, calls=%fused_computation.10 | convolution fusion | flops 50331776 | bytes 8651008 | tf_op jit(solution)/shard_map/bu,btk->utk/dot_general | solution.py:20
  357.0 7.7 %fusion.6 = f32[2,128,256]{2,0,1:T(2,128)S(1)} fusion(f32[64,128,256]{2,1,0:T(8,128)S(1)} %copy-done.4, s32[64]{0:T(128)S(1)} %get-tuple-element.6), kind=kOutput, calls=%fused_computation.12 | convolution fusion | flops 50331776 | bytes 8651008 | tf_op jit(solution)/shard_map/bu,btk->utk/dot_general | solution.py:40
  364.8 4.3 gather_fusion.4
  369.1 16.8 %fusion.41 = f32[64,128,128]{2,1,0:T(8,128)} fusion(f32[64,128,256]{2,1,0:T(8,128)} %gather_fusion.4, f32[64,128,256]{1,2,0:T(8,128)} %gather_fusion.2), kind=kOutput, calls=%fused_computation.88 | convolution fusion | flops 3221225472 | bytes 20971520 | tf_op jit(solution)/shard_map/btk,bik->bti/dot_general | solution.py:18
  385.9 15.7 %fusion.10 = f32[64,128,256]{2,1,0:T(8,128)} fusion(f32[64,128,256]{1,2,0:T(8,128)} %gather_fusion.2, f32[64,128,128]{2,1,0:T(8,128)} %fusion.41, f32[64,128,128]{2,1,0:T(8,128)S(1)} %copy-done.2, f32[64]{0:T(128)S(1)} %compare_convert_fusion), kind=kOutput, calls=%fused_computation.17 | convolution fusion | flops 3223322624 | bytes 25166080 | tf_op jit(solution)/shard_map/bti,bik->btk/dot_general | solution.py:19
  401.6 10.6 %fusion.2 = f32[2,128,256]{2,0,1:T(2,128)S(1)} fusion(f32[64,128,256]{2,1,0:T(8,128)} %fusion.10, s32[64]{0:T(128)S(1)} %get-tuple-element.6), kind=kOutput, calls=%fused_computation.8 | convolution fusion | flops 50331776 | bytes 8651008 | tf_op jit(solution)/shard_map/bu,btk->utk/dot_general | solution.py:20
  413.2 4.3 gather_fusion.5
  417.5 16.6 %fusion.42 = f32[64,128,128]{2,1,0:T(8,128)} fusion(f32[64,128,256]{2,1,0:T(8,128)} %gather_fusion.5, f32[64,128,256]{1,2,0:T(8,128)} %gather_fusion.2), kind=kOutput, calls=%fused_computation.89 | convolution fusion | flops 3221225472 | bytes 20971520 | tf_op jit(solution)/shard_map/btk,bik->bti/dot_general | solution.py:18
  434.1 15.7 %fusion.8 = f32[64,128,256]{2,1,0:T(8,128)} fusion(f32[64,128,256]{1,2,0:T(8,128)} %gather_fusion.2, f32[64,128,128]{2,1,0:T(8,128)} %fusion.42, f32[64,128,128]{2,1,0:T(8,128)S(1)} %copy-done.3, f32[64]{0:T(128)S(1)} %compare_convert_fusion), kind=kOutput, calls=%fused_computation.15 | convolution fusion | flops 3223322624 | bytes 25166080 | tf_op jit(solution)/shard_map/bti,bik->btk/dot_general | solution.py:19
  449.8 10.7 %fusion = f32[2,128,256]{2,0,1:T(2,128)S(1)} fusion(f32[64,128,256]{2,1,0:T(8,128)} %fusion.8, s32[64]{0:T(128)S(1)} %get-tuple-element.6), kind=kOutput, calls=%fused_computation.6 | convolution fusion | flops 50331776 | bytes 8651008 | tf_op jit(solution)/shard_map/bu,btk->utk/dot_general | solution.py:20
  461.1 4.4 broadcast_multiply_fusion
  465.5 5.6 all-to-all-start.3
  472.5 103.9 %all-to-all-done.3 = f32[32,256,256]{2,1,0:T(8,128)} async-done(((f32[32,256,256]{2,1,0:T(8,128)}), f32[32,256,256]{2,1,0:T(8,128)}, u32[]{:S(2)}, u32[]{:S(2)}) %all-to-all-start.3) | async-done | bytes 8388640 | tf_op jit(solution)/shard_map/all_to_all | solution.py:96
  576.4 111.6 %all-reduce.5.cloned.1.call-done = f32[256,256]{1,0:T(8,128)} async-done(((f32[256,256]{1,0:T(8,128)}), f32[256,256]{1,0:T(8,128)}) %all-reduce.5.cloned.1.call-update) | async-done | bytes 262160 | tf_op jit(solution)/shard_map/psum | solution.py:91
  689.6 7.7 %copy.159 = f32[1,32,256,256]{3,2,1,0:T(8,128)} copy(f32[1,32,256,256]{3,2,1,0:T(8,128)} %bitcast.23) | data formatting | bytes 16777216
  (52 shorter events, 9.6 us)
Async XLA Ops:
  10.2 21.3 %all-to-all-start = ((s32[128,1,2]{2,1,0:T(1,128)}), s32[128,1,2]{2,1,0:T(1,128)S(1)}, u32[]{:S(2)}, u32[]{:S(2)}) async-start(s32[128,1,2]{2,1,0:T(1,128)} %bitcast.6), calls=%async_computation | async-start | bytes 131072 | tf_op jit(solution)/shard_map/all_to_all | solution.py:83
  31.6 30.6 %all-to-all-start.2 = ((f32[4,2048,64]{1,2,0:T(8,128)}), f32[4,2048,64]{1,2,0:T(8,128)}, u32[]{:S(2)}, u32[]{:S(2)}) async-start(f32[4,2048,64]{1,2,0:T(8,128)} %bitcast.76), calls=%async_computation.2 | async-start | bytes 4194304 | tf_op jit(solution)/shard_map/all_to_all | solution.py:67
  62.1 6.9 copy-start.7
  62.1 7.0 copy-start.8
  62.1 11.9 %copy-start.1 = (f32[256,256]{1,0:T(8,128)S(1)}, f32[256,256]{1,0:T(8,128)}, u32[]{:S(2)}) copy-start(f32[256,256]{1,0:T(8,128)} %param.13) | copy-start | bytes 786436
  62.1 222.5 %all-to-all-start.1 = ((f32[128,2,128,64]{2,3,1,0:T(8,128)}), f32[128,2,128,64]{2,3,1,0:T(8,128)}, u32[]{:S(2)}, u32[]{:S(2)}) async-start(f32[128,2,128,64]{2,3,1,0:T(8,128)} %bitcast.82), calls=%async_computation.1 | async-start | bytes 16777216 | tf_op jit(solution)/shard_map/all_to_all | solution.py:85
  68.2 215.1 %all-reduce.3.cloned.1.call-start = ((), (), s32[]{:S(2)}) async-start(), calls=%async_computation.4 | async-start | bytes 524288 | tf_op jit(solution)/shard_map/psum | solution.py:69
  305.9 16.8 %copy-start = (f32[64,128,256]{1,2,0:T(8,128)S(1)}, f32[64,128,256]{1,2,0:T(8,128)}, u32[]{:S(2)}) copy-start(f32[64,128,256]{1,2,0:T(8,128)} %gather_fusion.2) | copy-start | bytes 25165828
  346.4 10.6 %copy-start.4 = (f32[64,128,256]{2,1,0:T(8,128)S(1)}, f32[64,128,256]{2,1,0:T(8,128)}, u32[]{:S(2)}) copy-start(f32[64,128,256]{2,1,0:T(8,128)} %fusion.14) | copy-start | bytes 25165828
  369.1 16.8 %copy-start.2 = (f32[64,128,128]{2,1,0:T(8,128)S(1)}, f32[64,128,128]{2,1,0:T(8,128)}, u32[]{:S(2)}) copy-start(f32[64,128,128]{2,1,0:T(8,128)} %param.12) | copy-start | bytes 12582916
  401.6 10.6 %copy-start.6 = (f32[256,256]{1,0:T(8,128)S(1)}, f32[256,256]{1,0:T(8,128)}, u32[]{:S(2)}) copy-start(f32[256,256]{1,0:T(8,128)} %all-reduce.3.cloned.1.call-done) | copy-start | bytes 786436
  417.5 16.6 %copy-start.3 = (f32[64,128,128]{2,1,0:T(8,128)S(1)}, f32[64,128,128]{2,1,0:T(8,128)}, u32[]{:S(2)}) copy-start(f32[64,128,128]{2,1,0:T(8,128)} %param.12) | copy-start | bytes 12582916
  461.1 10.0 %copy-start.5 = (f32[2,128,256]{2,1,0:T(8,128)}, f32[2,128,256]{2,1,0:T(8,128)S(1)}, u32[]{:S(2)}) copy-start(f32[2,128,256]{2,1,0:T(8,128)S(1)} %multiply_add_fusion) | copy-start | bytes 786436
  465.5 110.9 %all-to-all-start.3 = ((f32[32,256,256]{2,1,0:T(8,128)}), f32[32,256,256]{2,1,0:T(8,128)}, u32[]{:S(2)}, u32[]{:S(2)}) async-start(f32[32,256,256]{2,1,0:T(8,128)} %broadcast_multiply_fusion), calls=%async_computation.3 | async-start | bytes 16777216 | tf_op jit(solution)/shard_map/all_to_all | solution.py:96
  471.1 216.9 %all-reduce.5.cloned.1.call-start = ((), (), s32[]{:S(2)}) async-start(), calls=%async_computation.5 | async-start | bytes 524288 | tf_op jit(solution)/shard_map/psum | solution.py:91
Sparse Core Ops, SparseCore 0:
  74.3 208.9 all-reduce.2
  477.3 210.6 all-reduce.4
where the time goes:
time: 708 us; the launch traced here: 705 us
  waiting for transfers between devices  447 us (63%)
  matrix products  153 us (22%)
  local copies, waits for them, and re-layouts  53.9 us (8%)
  starting transfers between devices  27.8 us (4%)
  between operations  15.4 us (2%)
  other arithmetic  7.67 us (1%)
    psum x1, waiting for transfers between devices, body(): item_gram = lax.psum(partial_gram, ('wide', 'node'))  205 us
    psum x1, waiting for transfers between devices, body(): user_gram = lax.psum(partial_users, ('wide', 'node'))  112 us
    all_to_all x1, waiting for transfers between devices, body(): lax.all_to_all(outgoing_users, 'wide', split_axis=0, concat_axis=0, tiled...  104 us
    dot_general x3, matrix products, operate(): scores = jnp.einsum('btk,bik->bti', picked, picked_tiles, precision=highest)  50.3 us
    dot_general x3, matrix products, operate(): jnp.einsum('bti,bik->btk', scores * live_weights, picked_tiles, precision...  43.6 us
    dot_general x3, matrix products, operate(): local_term = jnp.einsum('bu,btk->utk', block_hot, spread, precision=highest)  31.8 us
    all_to_all x1, waiting for transfers between devices, body(): lax.all_to_all(item_factors, 'node', split_axis=0, concat_axis=1, tiled=T...  19.6 us
  transfers between devices with their start and end apart: 6, of which 5 were waited for; matrix products, arithmetic and copies ran while one was open for 3% of the time, Pallas kernels for 0%

commit v1 on v0

v1 whole, which is shorter than its diff:
```python
import functools

import jax
import jax.numpy as jnp
from jax import lax
from jax.experimental import pallas as pl
from jax.experimental.pallas import tpu as pltpu
from jax.sharding import PartitionSpec as P

TILE = 128
ITERS = 2
NEED = 32
K = 256
QUARTER = 64
NB = 64
WIDE = 32
NODE = 4
CORES = 2
PLANE = 16
SIDE = 4
TILES = 64
SHARE = 16
PAIRS = NEED // 2
PART = K // PLANE
RIDGE = 1.0
EPS = 1e-06

MESH = pl.DeviceIdType.MESH
F32 = jnp.float32
BF16 = jnp.bfloat16


def split(x):
    high = x.astype(BF16)
    return high, (x - high.astype(F32)).astype(BF16)


def dot3(a, b, contract):
    dims = ((contract[:1], contract[1:]), ((), ()))
    dot = lambda p, q: lax.dot_general(p, q, dims, preferred_element_type=F32)
    return dot(a[0], b[0]) + (dot(a[0], b[1]) + dot(a[1], b[0]))


def place_at():
    wide, node = lax.axis_index("wide"), lax.axis_index("node")
    return wide, node, wide // CORES, lax.rem(wide, CORES)


def remote(src, dst, send, recv, wide, node):
    return pltpu.make_async_remote_copy(
        src_ref=src, dst_ref=dst, send_sem=send, recv_sem=recv, device_id=(wide, node), device_id_type=MESH
    )


def each(low, high, step):
    lax.fori_loop(low, high, lambda i, c: (step(i), c)[1], 0)


def greet():
    wide, node, spot, core = place_at()
    barrier = pltpu.get_barrier_semaphore()

    def to_wide(k):
        pl.semaphore_signal(barrier, inc=1, device_id=(lax.rem(wide + k, WIDE), node), device_id_type=MESH)

    each(1, WIDE, to_wide)
    for dx in range(1, NODE):
        for dc in range(CORES):
            pl.semaphore_signal(
                barrier,
                inc=1,
                device_id=(spot * CORES + lax.rem(core + dc, CORES), lax.rem(node + dx, NODE)),
                device_id_type=MESH,
            )
    pl.semaphore_wait(barrier, WIDE - 1 + (NODE - 1) * CORES)


class Summer:
    def __init__(self, part, total, red, mid, sems):
        self.part, self.total, self.red, self.mid, self.sems = part, total, red, mid, sems
        self.wide, self.node, self.spot, self.core = place_at()
        self.eighth = self.node * CORES + self.core
        self.rows = pl.ds(pl.multiple_of(self.spot * PART, PART), PART)

    def over_plane(self, k, stage):
        spot = lax.rem(self.spot + k, PLANE)
        send, recv = self.sems.at[stage, 0, k], self.sems.at[stage, 1, k]
        if stage == 0:
            src = self.part.at[pl.ds(pl.multiple_of(spot * PART, PART), PART)]
            dst = self.red.at[self.spot]
        else:
            src = dst = self.total.at[self.rows]
        return remote(src, dst, send, recv, spot * CORES + self.core, self.node)

    def over_eight(self, k):
        other = lax.rem(self.eighth + k, NODE * CORES)
        slot = self.mid.at[self.eighth]
        wide = self.spot * CORES + lax.rem(other, CORES)
        return remote(slot, slot, self.sems.at[1, 0, k], self.sems.at[1, 1, k], wide, other // CORES)

    def first(self):
        each(1, PLANE, lambda k: self.over_plane(k, 0).start())
        self.red[self.spot] = self.part[self.rows, :]

    def second(self):
        each(1, PLANE, lambda k: self.over_plane(k, 0).wait_recv())
        total = self.red[0]
        for i in range(1, PLANE):
            total = total + self.red[i]
        self.mid[self.eighth] = total
        each(1, NODE * CORES, lambda k: self.over_eight(k).start())

    def third(self):
        each(1, NODE * CORES, lambda k: self.over_eight(k).wait_recv())
        total = self.mid[0]
        for i in range(1, NODE * CORES):
            total = total + self.mid[i]
        self.total[self.rows, :] = total
        each(1, PLANE, lambda k: self.over_plane(k, 2).start())

    def last(self):
        each(1, PLANE, lambda k: self.over_plane(k, 2).wait_recv())
        each(1, PLANE, lambda k: self.over_plane(k, 0).wait_send())
        each(1, NODE * CORES, lambda k: self.over_eight(k).wait_send())
        each(1, PLANE, lambda k: self.over_plane(k, 2).wait_send())


SUMMER_SCRATCH = [
    pltpu.VMEM((K, K), F32),
    pltpu.VMEM((PLANE, PART, K), F32),
    pltpu.VMEM((NODE * CORES, PART, K), F32),
    pltpu.SemaphoreType.DMA((3, 2, PLANE)),
]


def plan_kernel(owner, slot, index, count, req, place, where, seen):
    def clear(i):
        req[i] = -1
        where[i] = -1

    def clear_rest(i):
        req[i] = -1

    each(0, NB, clear)
    each(NB, TILE, clear_rest)
    each(0, WIDE, lambda i: seen.__setitem__(i, 0))

    def entry(e):
        o = owner[e]
        at = 2 * o + seen[o]
        seen[o] = seen[o] + 1
        place[e] = at
        req[at] = slot[e]

    each(0, NEED, entry)

    def block(b):
        where[index[b]] = b

    each(0, count[0], block)


def plan(owner, slot, index, count):
    smem = pl.BlockSpec(memory_space=pltpu.SMEM)
    return pl.pallas_call(
        plan_kernel,
        out_shape=[
            jax.ShapeDtypeStruct((TILE,), jnp.int32),
            jax.ShapeDtypeStruct((NEED,), jnp.int32),
            jax.ShapeDtypeStruct((NB,), jnp.int32),
        ],
        in_specs=[smem] * 4,
        out_specs=[smem] * 3,
        scratch_shapes=[pltpu.SMEM((WIDE,), jnp.int32)],
        name="plan",
    )(owner, slot, index, count)


def fetch_kernel(
    item, req, place, lists, gram, table,
    tiles, full, outbox, inbox, asked, part, red, mid, sum_sems, row_sems, ask_sems, tile_sems, ring_sems, load_sems, local_sem,
):
    wide, node, spot, core = place_at()

    def load(t):
        return pltpu.make_async_copy(
            item.at[:, pl.ds(pl.multiple_of(t * TILE, TILE), TILE)], tiles.at[t], load_sems.at[t]
        )

    each(0, TILES, lambda t: load(t).start())
    greet()

    def quarter(x):
        return pl.ds(pl.multiple_of(x * QUARTER, QUARTER), QUARTER)

    def share(x):
        return pl.ds(pl.multiple_of(x * SHARE, SHARE), SHARE)

    def rows_to(dx):
        x = lax.rem(node + dx, NODE)
        return remote(
            tiles.at[share(x)], full.at[:, quarter(node), :], row_sems.at[0, dx], row_sems.at[1, dx], wide, x
        )

    def ask(k):
        return remote(
            req, table.at[wide], ask_sems.at[0, k], ask_sems.at[1, k], lax.rem(wide + k, WIDE), node
        )

    def serve(k):
        other = lax.rem(wide + k, WIDE)
        return remote(
            outbox.at[other], inbox.at[pl.ds(2 * wide, 2)], tile_sems.at[0, k], tile_sems.at[1, k], other, node
        )

    each(1, WIDE, lambda k: ask(k).start())
    each(0, TILES, lambda t: load(t).wait())
    for dx in (1, 3, 2):
        rows_to(dx).start()
    table[wide] = req[...]
    full[:, quarter(node), :] = tiles[share(node)]
    each(1, WIDE, lambda k: ask(k).wait_recv())
    to_scalars = pltpu.make_async_copy(table, asked, local_sem)
    to_scalars.start()
    to_scalars.wait()

    def tile(other, r):
        return tiles[jnp.maximum(asked[other, 0, 2 * wide + r], 0)]

    def fill(k):
        other = lax.rem(wide + k, WIDE)
        for r in range(2):
            outbox[other, r] = tile(other, r)
        serve(k).start()

    each(1, WIDE, fill)
    for r in range(2):
        inbox[2 * wide + r] = tile(wide, r)

    for dx in (1, 3, 2):
        rows_to(dx).wait_recv()
    part[...] = jnp.zeros_like(part)

    def multiply(i):
        pair = split(jnp.concatenate([full[4 * i + j] for j in range(4)], axis=1))
        part[...] += dot3(pair, pair, (1, 1))

    each(0, SHARE // 4, multiply)
    summer = Summer(part, gram, red, mid, sum_sems)
    summer.first()

    each(1, WIDE, lambda k: serve(k).wait_recv())

    right, left = lax.rem(node + 1, NODE), lax.rem(node + NODE - 1, NODE)

    def pass_on(c, x, way):
        own = x is node
        stage = 0 if own else 1
        here = lists.at[pl.ds(2 * c, 2), quarter(x), :]
        return remote(
            here, here, ring_sems.at[stage, 0, way, c], ring_sems.at[stage, 1, way, c], wide, (right, left)[way]
        )

    def pick(c):
        for j in range(2):
            for r in range(2):
                lists[2 * c + j, quarter(node), r * TILE : (r + 1) * TILE] = inbox[place[4 * c + 2 * j + r]]
        pass_on(c, node, 0).start()
        pass_on(c, node, 1).start()

    each(0, 8, pick)
    summer.second()

    def forward(c):
        pass_on(2 * c, node, 0).wait_recv()
        pass_on(2 * c, left, 0).start()
        pass_on(2 * c + 1, node, 1).wait_recv()
        pass_on(2 * c + 1, right, 1).start()

    each(0, 2, forward)
    summer.third()
    each(2, 4, forward)

    def finish(c):
        pass_on(2 * c, node, 1).wait_recv()
        pass_on(2 * c + 1, node, 0).wait_recv()
        pass_on(2 * c, left, 0).wait()
        pass_on(2 * c + 1, right, 1).wait()

    each(0, 4, finish)
    summer.last()

    def drain(c):
        pass_on(c, node, 0).wait_send()
        pass_on(c, node, 1).wait_send()

    each(0, 8, drain)
    for dx in (1, 3, 2):
        rows_to(dx).wait_send()
    each(1, WIDE, lambda k: ask(k).wait_send())
    each(1, WIDE, lambda k: serve(k).wait_send())


def fetch(item, req, place):
    vmem = pl.BlockSpec(memory_space=pltpu.VMEM)
    smem = pl.BlockSpec(memory_space=pltpu.SMEM)
    return pl.pallas_call(
        fetch_kernel,
        out_shape=[
            jax.ShapeDtypeStruct((PAIRS, K, 2 * TILE), F32),
            jax.ShapeDtypeStruct((K, K), F32),
            jax.ShapeDtypeStruct((WIDE, 1, TILE), jnp.int32),
        ],
        in_specs=[pl.BlockSpec(memory_space=pl.ANY), vmem, smem],
        out_specs=[vmem, vmem, vmem],
        scratch_shapes=[
            pltpu.VMEM((TILES, QUARTER, TILE), F32),
            pltpu.VMEM((SHARE, K, TILE), F32),
            pltpu.VMEM((WIDE, 2, QUARTER, TILE), F32),
            pltpu.VMEM((2 * WIDE, QUARTER, TILE), F32),
            pltpu.SMEM((WIDE, 1, TILE), jnp.int32),
            *SUMMER_SCRATCH,
            pltpu.SemaphoreType.DMA((2, NODE)),
            pltpu.SemaphoreType.DMA((2, WIDE)),
            pltpu.SemaphoreType.DMA((2, WIDE)),
            pltpu.SemaphoreType.DMA((2, 2, 2, 8)),
            pltpu.SemaphoreType.DMA((TILES,)),
            pltpu.SemaphoreType.DMA,
        ],
        compiler_params=pltpu.CompilerParams(
            collective_id=0, has_side_effects=True, vmem_limit_bytes=40 * 1024 * 1024
        ),
        name="fetch",
    )(item, req, place)


def solve_kernel(lists, weights, user, gram, where, users_new, partial, high, low, dense, spread):
    x = user[...]
    gram_pair = split(gram[...])

    def globally(d, pair):
        return dot3(pair, gram_pair, (1, 0)) + RIDGE * d

    xs = split(x)
    spread[...] = jnp.zeros_like(spread)

    def start(p):
        v = split(lists[p])
        high[p], low[p] = v
        s = dot3(xs, v, (1, 0))
        rows = []
        for u in range(2):
            cols = []
            for r in range(2):
                at = where[u * NEED + 2 * p + r]
                live = jnp.where(at >= 0, 1.0, 0.0).astype(F32)
                c = weights[jnp.maximum(at, 0)] * live
                dense[p, u * TILE : (u + 1) * TILE, r * TILE : (r + 1) * TILE] = c
                cols.append((c + live) - c * s[u * TILE : (u + 1) * TILE, r * TILE : (r + 1) * TILE])
            rows.append(jnp.concatenate(cols, axis=1))
        t = jnp.concatenate(rows, axis=0)
        spread[...] += dot3(split(t), v, (1, 1))

    each(0, PAIRS, start)
    residual = spread[...] - globally(x, xs)
    direction = residual
    norm = jnp.sum(residual * residual, axis=1, keepdims=True)

    pair = split(direction)
    spread[...] = jnp.zeros_like(spread)

    def apply(p):
        v = (high[p], low[p])
        t = dot3(pair, v, (1, 0)) * dense[p]
        spread[...] += dot3(split(t), v, (1, 1))

    each(0, PAIRS, apply)
    applied = spread[...] + globally(direction, pair)
    step = norm / (jnp.sum(direction * applied, axis=1, keepdims=True) + EPS)
    x = x + step * direction
    residual = residual - step * applied
    following = jnp.sum(residual * residual, axis=1, keepdims=True)
    direction = residual + following / (norm + EPS) * direction
    norm = following

    pair = split(direction)
    spread[...] = jnp.zeros_like(spread)

    def curve(p):
        s = dot3(pair, (high[p], low[p]), (1, 0))
        spread[...] += s * s * dense[p]

    each(0, PAIRS, curve)
    bend = spread[...] + direction * globally(direction, pair)
    step = norm / (jnp.sum(bend, axis=1, keepdims=True) + EPS)
    x = x + step * direction
    users_new[...] = x
    pair = split(x)
    partial[...] = dot3(pair, pair, (0, 0))


def solve(lists, weights, user, gram, where):
    vmem = pl.BlockSpec(memory_space=pltpu.VMEM)
    smem = pl.BlockSpec(memory_space=pltpu.SMEM)
    return pl.pallas_call(
        solve_kernel,
        out_shape=[jax.ShapeDtypeStruct((K, K), F32)] * 2,
        in_specs=[vmem] * 4 + [smem],
        out_specs=[vmem] * 2,
        scratch_shapes=[
            pltpu.VMEM((PAIRS, K, 2 * TILE), BF16),
            pltpu.VMEM((PAIRS, K, 2 * TILE), BF16),
            pltpu.VMEM((PAIRS, K, 2 * TILE), F32),
            pltpu.VMEM((K, K), F32),
        ],
        compiler_params=pltpu.CompilerParams(vmem_limit_bytes=40 * 1024 * 1024),
        name="solve",
    )(lists, weights, user, gram, where)


HALF = 128
BIT = 64


def deliver_kernel(
    users, partial, boxes, user_gram, part, red, mid, sum_sems, line_sems, cross_sems, sib_sems, local_sem
):
    wide, node, spot, core = place_at()
    y, z = spot // SIDE, lax.rem(spot, SIDE)
    greet()
    summer = Summer(partial, user_gram, red, mid, sum_sems)
    summer.first()

    def turn(a, d):
        return lax.rem(a + (d + SIDE), SIDE)

    def block(dy, dz):
        return (turn(y, dy) * SIDE + turn(z, dz)) * CORES + core

    def neighbour(axis, way):
        d = 1 if way == 0 else -1
        return block(d, 0) if axis == 0 else block(0, d)

    def rows(half, bit):
        if bit is None:
            return pl.ds(half * HALF, HALF)
        return pl.ds(half * HALF + bit * BIT, BIT)

    def line(half, way, far):
        axis = half
        d = 0 if not far else (-1 if way == 0 else 1)
        at = block(d, 0) if axis == 0 else block(0, d)
        r = rows(half, way if far else None)
        src = users.at[r] if not far else boxes.at[at, r]
        return remote(
            src, boxes.at[at, r], line_sems.at[0, half, way, far], line_sems.at[1, half, way, far],
            neighbour(axis, way), node,
        )

    def cross(half, along, way, far):
        axis = 1 - half
        d = 0 if not far else (-1 if way == 0 else 1)
        at = block(along, d) if axis == 1 else block(d, along)
        r = rows(half, way if far else None)
        src = users.at[r] if (not far and along == 0) else boxes.at[at, r]
        return remote(
            src, boxes.at[at, r],
            cross_sems.at[0, half, along % SIDE, way, far], cross_sems.at[1, half, along % SIDE, way, far],
            neighbour(axis, way), node,
        )

    def sibling(half, along, over):
        at = block(along, over) if half == 0 else block(over, along)
        r = rows(half, None)
        src = users.at[r] if (along == 0 and over == 0) else boxes.at[at, r]
        i = (along % SIDE) * SIDE + over % SIDE
        return remote(
            src, boxes.at[at, r], sib_sems.at[0, half, i], sib_sems.at[1, half, i],
            spot * CORES + 1 - core, node,
        )

    own = pltpu.make_async_copy(users, boxes.at[wide], local_sem)
    own.start()
    for half in range(2):
        for way in range(2):
            line(half, way, 0).start()
    for half in range(2):
        for way in range(2):
            cross(half, 0, way, 0).start()
    for half in range(2):
        sibling(half, 0, 0).start()

    def come_from(way):
        return -1 if way == 0 else 1

    for way in range(2):
        for half in range(2):
            line(half, way, 0).wait_recv()
            line(half, way, 1).start()
            for w in range(2):
                cross(half, come_from(way), w, 0).start()
            sibling(half, come_from(way), 0).start()
    summer.second()
    for half in range(2):
        for way in range(2):
            line(half, way, 1).wait_recv()
        for w in range(2):
            cross(half, 2, w, 0).start()
        sibling(half, 2, 0).start()
    summer.third()
    for along in (0, -1, 1, 2):
        for half in range(2):
            for way in range(2):
                cross(half, along, way, 0).wait_recv()
                cross(half, along, way, 1).start()
                sibling(half, along, come_from(way)).start()
    summer.last()
    for along in (0, -1, 1, 2):
        for half in range(2):
            for way in range(2):
                cross(half, along, way, 1).wait_recv()
            sibling(half, along, 2).start()
    for along in (0, -1, 1, 2):
        for half in range(2):
            for over in (0, -1, 1, 2):
                sibling(half, along, over).wait()
            for way in range(2):
                for far in range(2):
                    cross(half, along, way, far).wait_send()
    for half in range(2):
        for way in range(2):
            for far in range(2):
                line(half, way, far).wait_send()
    own.wait()


def deliver(users, partial):
    vmem = pl.BlockSpec(memory_space=pltpu.VMEM)
    return pl.pallas_call(
        deliver_kernel,
        out_shape=[
            jax.ShapeDtypeStruct((WIDE, K, K), F32),
            jax.ShapeDtypeStruct((K, K), F32),
        ],
        in_specs=[vmem, vmem],
        out_specs=[pl.BlockSpec(memory_space=pl.ANY), vmem],
        scratch_shapes=[
            *SUMMER_SCRATCH,
            pltpu.SemaphoreType.DMA((2, 2, 2, 2)),
            pltpu.SemaphoreType.DMA((2, 2, SIDE, 2, 2)),
            pltpu.SemaphoreType.DMA((2, 2, PLANE)),
            pltpu.SemaphoreType.DMA,
        ],
        compiler_params=pltpu.CompilerParams(collective_id=1, has_side_effects=True),
        name="deliver",
    )(users, partial)


def mask_kernel(table, boxes, out):
    wide = lax.axis_index("wide")
    for j in range(4):
        named = table[pl.program_id(0) * 4 + j, 0, 2 * wide] >= 0
        out[0, j] = jnp.where(named, boxes[j], 0.0)


def mask(table, boxes):
    return pl.pallas_call(
        mask_kernel,
        grid=(WIDE // 4,),
        out_shape=jax.ShapeDtypeStruct((1, WIDE, K, K), F32),
        in_specs=[pl.BlockSpec(memory_space=pltpu.SMEM), pl.BlockSpec((4, K, K), lambda g: (g, 0, 0))],
        out_specs=pl.BlockSpec((1, 4, K, K), lambda g: (0, g, 0, 0)),
        name="mask",
    )(table, boxes)


def body(item_factors, need_owner, need_slot, block_index, block_count, weights, user_old):
    req, place, where = plan(need_owner[:, 0], need_slot, block_index, block_count)
    lists, gram, table = fetch(item_factors.T, req.reshape(1, TILE), place)
    users_new, partial = solve(lists, weights, user_old, gram, where)
    boxes, user_gram = deliver(users_new, partial)
    return users_new, user_gram, mask(table, boxes)


def solution(mesh):
    placed = (
        P("wide", "node"),
        P("wide", None),
        P("wide"),
        P(("wide", "node")),
        P(("wide", "node")),
        P(("wide", "node"), None, None),
        P(("wide", "node"), None),
    )
    return jax.shard_map(
        body,
        mesh=mesh,
        in_specs=placed,
        out_specs=(P(("wide", "node"), None), P(), P("wide", None, "node", None)),
        check_vma=False,
    )
```

time: 708 us -> 189 us (0.27)
  waiting for transfers between devices: 447 us -> 0 us
  Pallas kernels: 0 us -> 179 us
  matrix products: 153 us -> 0 us
  local copies, waits for them, and re-layouts: 53.9 us -> 8.68 us
  starting transfers between devices: 27.8 us -> 0 us
  between operations: 15.4 us -> 1.33 us
  other arithmetic: 7.67 us -> 0 us
    psum x2 -> x0, waiting for transfers between devices: 316 us -> none  [the longest x1 205 us: body(): item_gram = lax.psum(partial_gram, ('wide', 'node'))]
    pallas_call x0 -> x5, Pallas kernels: none -> 179 us  [the longest x1 96.4 us: fetch(): pl.pallas_call(fetch_kernel, out_shape=[jax.ShapeDtypeStruct((PAIRS, K, 2...]
    dot_general x16 -> x0, matrix products: 153 us -> none  [the longest x3 50.3 us: operate(): scores = jnp.einsum('btk,bik->bti', picked, picked_tiles, precision=highest)]
    all_to_all x4 -> x0, waiting for transfers between devices: 130 us -> none  [the longest x1 104 us: body(): lax.all_to_all(outgoing_users, 'wide', split_axis=0, concat_axis=0, tiled...]
    gather x6 -> x0, local copies, waits for them, and re-layouts: 30.3 us -> none  [the longest x3 12.9 us: operate(): picked = direction[tile_of_block]]
    all_to_all x4 -> x0, starting transfers between devices: 27.5 us -> none  [the longest x1 11.5 us: body(): lax.all_to_all(outgoing, ('wide', 'node'), split_axis=0, concat_axis=0, t...]
    transpose x1 -> x0, local copies, waits for them, and re-layouts: 8.44 us -> none  [body(): arrived.transpose(0, 2, 3, 1, 4)]
  transfers between devices with their start and end apart: 6 -> 0, of which waited for: 5 -> 0; matrix products, arithmetic and copies ran while one was open for 3% -> 0% of each run, Pallas kernels for 0% -> 0%
where the time goes in v1:
time: 189 us
  Pallas kernels  179 us (95%)
  local copies, waits for them, and re-layouts  8.68 us (5%)
    pallas_call x1, Pallas kernels, fetch(): pl.pallas_call(fetch_kernel, out_shape=[jax.ShapeDtypeStruct((PAIRS, K, 2...  96.4 us
    pallas_call x1, Pallas kernels, deliver(): pl.pallas_call(deliver_kernel, out_shape=[jax.ShapeDtypeStruct((WIDE, K,...  43.7 us
    pallas_call x1, Pallas kernels, solve(): pl.pallas_call(solve_kernel, out_shape=[jax.ShapeDtypeStruct((K, K), F32)...  26.5 us
    pallas_call x1, Pallas kernels, mask(): pl.pallas_call(mask_kernel, grid=(WIDE // 4,), out_shape=jax.ShapeDtypeSt...  9.33 us
    unnamed x19, local copies, waits for them, and re-layouts  8.68 us

profile of v1, /device:TPU:1, one launch (start us, length us, event | category | flops | bytes accessed | tf_op | source)
XLA Modules:
  0.0 189.0 jit_solution(11729125410556472449)
XLA Ops:
  1.3 3.0 %plan.1 = (s32[128]{0:T(128)}, s32[32]{0:T(128)}, s32[64]{0:T(128)}) custom-call(s32[32]{0:T(128)} %bitcast.5, s32[32]{0:T(128)} %slot.1, s32[64]{0:T(128)} %index.1, s32[1]{0:T(128)S(6)} %copy.11.count), custom_call_target="tpu_custom_call" | custom-call | tf_op jit(solution)/shard_map/plan/pallas_call | solution.py:165
  4.3 0.0 copy-start.1
  4.3 1.6 copy-done.1
  5.9 0.0 copy-start.6
  5.9 0.7 copy-done.6
  6.5 0.0 copy-start.7
  6.5 0.7 copy-done.7
  7.2 96.4 %fetch.1 = (f32[16,256,256]{2,1,0:T(8,128)S(1)}, f32[256,256]{1,0:T(8,128)S(1)}, s32[32,1,128]{2,1,0:T(1,128)S(1)}) custom-call(f32[64,8192]{1,0:T(8,128)S(1)} %bitcast.3, s32[1,128]{1,0:T(1,128)S(1)} %bitcast.4, s32[32]{0:T(128)S(1)} %copy-done.7), custom_call_target="tpu_custom_call" | custom-call | tf_op jit(solution)/shard_map/fetch/pallas_call | solution.py:307
  103.6 0.0 copy-start.4
  103.6 0.6 copy-done.4
  104.2 0.0 copy-start
  104.2 2.2 %copy-done = f32[64,128,128]{2,1,0:T(8,128)S(1)} copy-done((f32[64,128,128]{2,1,0:T(8,128)S(1)}, f32[64,128,128]{2,1,0:T(8,128)}, u32[]{:S(2)}) %copy-start) | copy-done | bytes 4194328
  106.4 0.0 copy-start.2
  106.4 0.9 copy-done.2
  107.3 0.0 copy-start.5
  107.3 0.7 copy-done.5
  108.0 26.5 %solve.1 = (f32[256,256]{1,0:T(8,128)}, f32[256,256]{1,0:T(8,128)S(1)}) custom-call(f32[16,256,256]{2,1,0:T(8,128)S(1)} %get-tuple-element.15.lists, f32[64,128,128]{2,1,0:T(8,128)S(1)} %copy-done, f32[256,256]{1,0:T(8,128)S(1)} %copy-done.2, f32[256,256]{1,0:T(8,128)S(1)} %get-tuple-element.16.gram, s32[64]{0:T(128)S(1)} %copy-done.5), custom_call_target="tpu_custom_call" | custom-call | tf_op jit(solution)/shard_map/solve/pallas_call | solution.py:405
  134.5 0.0 copy-start.3
  134.5 0.7 copy-done.3
  135.2 43.7 %deliver.1 = (f32[32,256,256]{2,1,0:T(8,128)}, f32[256,256]{1,0:T(8,128)}) custom-call(f32[256,256]{1,0:T(8,128)} %get-tuple-element.26.users, f32[256,256]{1,0:T(8,128)} %copy-done.3), custom_call_target="tpu_custom_call" | custom-call | tf_op jit(solution)/shard_map/deliver/pallas_call | solution.py:539
  178.9 0.0 copy-start.8
  178.9 9.3 %mask.1 = f32[1,32,256,256]{3,2,1,0:T(8,128)} custom-call(s32[32,1,128]{2,1,0:T(1,128)} %copy-done.4, f32[32,256,256]{2,1,0:T(8,128)} %get-tuple-element.22.boxes), custom_call_target="tpu_custom_call" | custom-call | tf_op jit(solution)/shard_map/mask/pallas_call | solution.py:567
  188.3 0.0 copy-done.8
  188.3 0.7 copy.12
Async XLA Ops:
  4.3 1.6 copy-start.1
  5.9 0.7 copy-start.6
  6.5 0.7 copy-start.7
  103.6 0.6 copy-start.4
  104.2 2.2 %copy-start = (f32[64,128,128]{2,1,0:T(8,128)S(1)}, f32[64,128,128]{2,1,0:T(8,128)}, u32[]{:S(2)}) copy-start(f32[64,128,128]{2,1,0:T(8,128)} %weights.1) | copy-start | bytes 12582916
  106.4 0.9 copy-start.2
  107.3 0.7 copy-start.5
  134.5 0.7 copy-start.3
  178.9 9.3 %copy-start.8 = (f32[256,256]{1,0:T(8,128)S(1)}, f32[256,256]{1,0:T(8,128)}, u32[]{:S(2)}) copy-start(f32[256,256]{1,0:T(8,128)} %get-tuple-element.27) | copy-start | bytes 786436

commit v2 on v1

--- a/solution.py
+++ b/solution.py
@@ -21,6 +21,11 @@
 TILES = 64
 SHARE = 16
 PAIRS = NEED // 2
+GROUP = 4
+STEPS = PAIRS // GROUP
+SPAN = GROUP * 2 * TILE
+HALF = 128
+BIT = 64
 PART = K // PLANE
 RIDGE = 1.0
 EPS = 1e-06
@@ -35,10 +40,14 @@
     return high, (x - high.astype(F32)).astype(BF16)
 
 
+def dot(a, b, contract):
+    return lax.dot_general(a, b, ((contract[:1], contract[1:]), ((), ())), preferred_element_type=F32)
+
+
 def dot3(a, b, contract):
-    dims = ((contract[:1], contract[1:]), ((), ()))
-    dot = lambda p, q: lax.dot_general(p, q, dims, preferred_element_type=F32)
-    return dot(a[0], b[0]) + (dot(a[0], b[1]) + dot(a[1], b[0]))
+    left = jnp.concatenate([a[0], a[0], a[1]], axis=contract[0])
+    right = jnp.concatenate([b[0], b[1], b[0]], axis=contract[1])
+    return dot(left, right, contract)
 
 
 def place_at():
@@ -123,14 +132,6 @@
         each(1, PLANE, lambda k: self.over_plane(k, 0).wait_send())
         each(1, NODE * CORES, lambda k: self.over_eight(k).wait_send())
         each(1, PLANE, lambda k: self.over_plane(k, 2).wait_send())
-
-
-SUMMER_SCRATCH = [
-    pltpu.VMEM((K, K), F32),
-    pltpu.VMEM((PLANE, PART, K), F32),
-    pltpu.VMEM((NODE * CORES, PART, K), F32),
-    pltpu.SemaphoreType.DMA((3, 2, PLANE)),
-]
 
 
 def plan_kernel(owner, slot, index, count, req, place, where, seen):
@@ -176,9 +177,12 @@
     )(owner, slot, index, count)
 
 
-def fetch_kernel(
-    item, req, place, lists, gram, table,
-    tiles, full, outbox, inbox, asked, part, red, mid, sum_sems, row_sems, ask_sems, tile_sems, ring_sems, load_sems, local_sem,
+def step_kernel(
+    item, req, place, where, weights_in, user_in,
+    users_new, user_gram, boxes, table,
+    tiles, full, outbox, inbox, asked, lists, weights, user, users, gram, part, red, mid, high, low, dense, spread,
+    sum_sems, row_sems, ask_sems, tile_sems, ring_sems, line_sems, cross_sems, sib_sems,
+    load_sems, bring_sems, own_sems, local_sem,
 ):
     wide, node, spot, core = place_at()
 
@@ -188,6 +192,10 @@
         )
 
     each(0, TILES, lambda t: load(t).start())
+    bring_weights = pltpu.make_async_copy(weights_in, weights, bring_sems.at[0])
+    bring_user = pltpu.make_async_copy(user_in, user, bring_sems.at[1])
+    bring_weights.start()
+    bring_user.start()
     greet()
 
     def quarter(x):
@@ -246,7 +254,7 @@
         part[...] += dot3(pair, pair, (1, 1))
 
     each(0, SHARE // 4, multiply)
-    summer = Summer(part, gram, red, mid, sum_sems)
+    summer = Summer(part, gram, red.at[0], mid.at[0], sum_sems.at[0])
     summer.first()
 
     each(1, WIDE, lambda k: serve(k).wait_recv())
@@ -280,101 +288,59 @@
     each(0, 2, forward)
     summer.third()
     each(2, 4, forward)
-
-    def finish(c):
+    bring_weights.wait()
+    bring_user.wait()
+
+    x = user[...]
+    pair = split(x)
+    spread[...] = jnp.zeros_like(spread)
+
+    def arrive(c):
         pass_on(2 * c, node, 1).wait_recv()
         pass_on(2 * c + 1, node, 0).wait_recv()
-        pass_on(2 * c, left, 0).wait()
-        pass_on(2 * c + 1, right, 1).wait()
-
-    each(0, 4, finish)
-    summer.last()
-
-    def drain(c):
-        pass_on(c, node, 0).wait_send()
-        pass_on(c, node, 1).wait_send()
-
-    each(0, 8, drain)
-    for dx in (1, 3, 2):
-        rows_to(dx).wait_send()
-    each(1, WIDE, lambda k: ask(k).wait_send())
-    each(1, WIDE, lambda k: serve(k).wait_send())
-
-
-def fetch(item, req, place):
-    vmem = pl.BlockSpec(memory_space=pltpu.VMEM)
-    smem = pl.BlockSpec(memory_space=pltpu.SMEM)
-    return pl.pallas_call(
-        fetch_kernel,
-        out_shape=[
-            jax.ShapeDtypeStruct((PAIRS, K, 2 * TILE), F32),
-            jax.ShapeDtypeStruct((K, K), F32),
-            jax.ShapeDtypeStruct((WIDE, 1, TILE), jnp.int32),
-        ],
-        in_specs=[pl.BlockSpec(memory_space=pl.ANY), vmem, smem],
-        out_specs=[vmem, vmem, vmem],
-        scratch_shapes=[
-            pltpu.VMEM((TILES, QUARTER, TILE), F32),
-            pltpu.VMEM((SHARE, K, TILE), F32),
-            pltpu.VMEM((WIDE, 2, QUARTER, TILE), F32),
-            pltpu.VMEM((2 * WIDE, QUARTER, TILE), F32),
-            pltpu.SMEM((WIDE, 1, TILE), jnp.int32),
-            *SUMMER_SCRATCH,
-            pltpu.SemaphoreType.DMA((2, NODE)),
-            pltpu.SemaphoreType.DMA((2, WIDE)),
-            pltpu.SemaphoreType.DMA((2, WIDE)),
-            pltpu.SemaphoreType.DMA((2, 2, 2, 8)),
-            pltpu.SemaphoreType.DMA((TILES,)),
-            pltpu.SemaphoreType.DMA,
-        ],
-        compiler_params=pltpu.CompilerParams(
-            collective_id=0, has_side_effects=True, vmem_limit_bytes=40 * 1024 * 1024
-        ),
-        name="fetch",
-    )(item, req, place)
-
-
-def solve_kernel(lists, weights, user, gram, where, users_new, partial, high, low, dense, spread):
-    x = user[...]
-    gram_pair = split(gram[...])
-
-    def globally(d, pair):
-        return dot3(pair, gram_pair, (1, 0)) + RIDGE * d
-
-    xs = split(x)
-    spread[...] = jnp.zeros_like(spread)
-
-    def start(p):
-        v = split(lists[p])
-        high[p], low[p] = v
-        s = dot3(xs, v, (1, 0))
+        pass_on(2 * c, left, 0).wait_recv()
+        pass_on(2 * c + 1, right, 1).wait_recv()
+
+    def begin(i):
+        arrive(i)
+        parts = [split(lists[GROUP * i + j]) for j in range(GROUP)]
+        v = tuple(jnp.concatenate([q[k] for q in parts], axis=1) for k in range(2))
+        high[i], low[i] = v
+        s = dot3(pair, v, (1, 0))
         rows = []
         for u in range(2):
             cols = []
-            for r in range(2):
-                at = where[u * NEED + 2 * p + r]
-                live = jnp.where(at >= 0, 1.0, 0.0).astype(F32)
+            for r in range(2 * GROUP):
+                at = where[u * NEED + 2 * GROUP * i + r]
+                live = (jnp.minimum(at, 0) + 1).astype(F32)
                 c = weights[jnp.maximum(at, 0)] * live
-                dense[p, u * TILE : (u + 1) * TILE, r * TILE : (r + 1) * TILE] = c
-                cols.append((c + live) - c * s[u * TILE : (u + 1) * TILE, r * TILE : (r + 1) * TILE])
+                here = slice(u * TILE, (u + 1) * TILE), slice(r * TILE, (r + 1) * TILE)
+                dense[i, here[0], here[1]] = c
+                cols.append((c + live) - c * s[here])
             rows.append(jnp.concatenate(cols, axis=1))
-        t = jnp.concatenate(rows, axis=0)
-        spread[...] += dot3(split(t), v, (1, 1))
-
-    each(0, PAIRS, start)
-    residual = spread[...] - globally(x, xs)
+        spread[...] += dot3(split(jnp.concatenate(rows, axis=0)), v, (1, 1))
+
+    each(0, STEPS, begin)
+    summer.last()
+
+    gram_pair = split(gram[...])
+
+    def globally(d, pair):
+        return dot3(pair, gram_pair, (1, 0)) + RIDGE * d
+
+    residual = spread[...] - globally(x, pair)
     direction = residual
     norm = jnp.sum(residual * residual, axis=1, keepdims=True)
 
     pair = split(direction)
     spread[...] = jnp.zeros_like(spread)
 
-    def apply(p):
-        v = (high[p], low[p])
-        t = dot3(pair, v, (1, 0)) * dense[p]
+    def apply(i):
+        v = (high[i], low[i])
+        t = dot3(pair, v, (1, 0)) * dense[i]
         spread[...] += dot3(split(t), v, (1, 1))
 
-    each(0, PAIRS, apply)
+    each(0, STEPS, apply)
     applied = spread[...] + globally(direction, pair)
     step = norm / (jnp.sum(direction * applied, axis=1, keepdims=True) + EPS)
     x = x + step * direction
@@ -384,53 +350,22 @@
     norm = following
 
     pair = split(direction)
-    spread[...] = jnp.zeros_like(spread)
-
-    def curve(p):
-        s = dot3(pair, (high[p], low[p]), (1, 0))
-        spread[...] += s * s * dense[p]
-
-    each(0, PAIRS, curve)
-    bend = spread[...] + direction * globally(direction, pair)
-    step = norm / (jnp.sum(bend, axis=1, keepdims=True) + EPS)
+    spread[...] = direction * globally(direction, pair)
+
+    def curve(i):
+        s = dot3(pair, (high[i], low[i]), (1, 0))
+        bend = s * s * dense[i]
+        total = spread[...]
+        for j in range(GROUP):
+            total = total + bend[:, j * 2 * TILE : (j + 1) * 2 * TILE]
+        spread[...] = total
+
+    each(0, STEPS, curve)
+    step = norm / (jnp.sum(spread[...], axis=1, keepdims=True) + EPS)
     x = x + step * direction
-    users_new[...] = x
-    pair = split(x)
-    partial[...] = dot3(pair, pair, (0, 0))
-
-
-def solve(lists, weights, user, gram, where):
-    vmem = pl.BlockSpec(memory_space=pltpu.VMEM)
-    smem = pl.BlockSpec(memory_space=pltpu.SMEM)
-    return pl.pallas_call(
-        solve_kernel,
-        out_shape=[jax.ShapeDtypeStruct((K, K), F32)] * 2,
-        in_specs=[vmem] * 4 + [smem],
-        out_specs=[vmem] * 2,
-        scratch_shapes=[
-            pltpu.VMEM((PAIRS, K, 2 * TILE), BF16),
-            pltpu.VMEM((PAIRS, K, 2 * TILE), BF16),
-            pltpu.VMEM((PAIRS, K, 2 * TILE), F32),
-            pltpu.VMEM((K, K), F32),
-        ],
-        compiler_params=pltpu.CompilerParams(vmem_limit_bytes=40 * 1024 * 1024),
-        name="solve",
-    )(lists, weights, user, gram, where)
-
-
-HALF = 128
-BIT = 64
-
-
-def deliver_kernel(
-    users, partial, boxes, user_gram, part, red, mid, sum_sems, line_sems, cross_sems, sib_sems, local_sem
-):
-    wide, node, spot, core = place_at()
+    users[...] = x
+
     y, z = spot // SIDE, lax.rem(spot, SIDE)
-    greet()
-    summer = Summer(partial, user_gram, red, mid, sum_sems)
-    summer.first()
-
     def turn(a, d):
         return lax.rem(a + (d + SIDE), SIDE)
 
@@ -479,8 +414,10 @@
             spot * CORES + 1 - core, node,
         )
 
-    own = pltpu.make_async_copy(users, boxes.at[wide], local_sem)
+    own = pltpu.make_async_copy(users, boxes.at[wide], own_sems.at[0])
     own.start()
+    give = pltpu.make_async_copy(users, users_new, own_sems.at[1])
+    give.start()
     for half in range(2):
         for way in range(2):
             line(half, way, 0).start()
@@ -489,6 +426,11 @@
             cross(half, 0, way, 0).start()
     for half in range(2):
         sibling(half, 0, 0).start()
+
+    pair = split(x)
+    part[...] = dot3(pair, pair, (0, 0))
+    summer = Summer(part, user_gram, red.at[1], mid.at[1], sum_sems.at[1])
+    summer.first()
 
     def come_from(way):
         return -1 if way == 0 else 1
@@ -532,28 +474,75 @@
             for far in range(2):
                 line(half, way, far).wait_send()
     own.wait()
-
-
-def deliver(users, partial):
+    give.wait()
+
+    def drain(c):
+        pass_on(c, node, 0).wait_send()
+        pass_on(c, node, 1).wait_send()
+
+    each(0, 8, drain)
+
+    def drain_far(c):
+        pass_on(2 * c, left, 0).wait_send()
+        pass_on(2 * c + 1, right, 1).wait_send()
+
+    each(0, 4, drain_far)
+    for dx in (1, 3, 2):
+        rows_to(dx).wait_send()
+    each(1, WIDE, lambda k: ask(k).wait_send())
+    each(1, WIDE, lambda k: serve(k).wait_send())
+
+
+def step(item, req, place, where, weights, user):
     vmem = pl.BlockSpec(memory_space=pltpu.VMEM)
+    smem = pl.BlockSpec(memory_space=pltpu.SMEM)
+    hbm = pl.BlockSpec(memory_space=pl.ANY)
     return pl.pallas_call(
-        deliver_kernel,
+        step_kernel,
         out_shape=[
+            jax.ShapeDtypeStruct((K, K), F32),
+            jax.ShapeDtypeStruct((K, K), F32),
             jax.ShapeDtypeStruct((WIDE, K, K), F32),
-            jax.ShapeDtypeStruct((K, K), F32),
+            jax.ShapeDtypeStruct((WIDE, 1, TILE), jnp.int32),
         ],
-        in_specs=[vmem, vmem],
-        out_specs=[pl.BlockSpec(memory_space=pl.ANY), vmem],
+        in_specs=[hbm, vmem, smem, smem, hbm, hbm],
+        out_specs=[hbm, vmem, hbm, vmem],
         scratch_shapes=[
-            *SUMMER_SCRATCH,
+            pltpu.VMEM((TILES, QUARTER, TILE), F32),
+            pltpu.VMEM((SHARE, K, TILE), F32),
+            pltpu.VMEM((WIDE, 2, QUARTER, TILE), F32),
+            pltpu.VMEM((2 * WIDE, QUARTER, TILE), F32),
+            pltpu.SMEM((WIDE, 1, TILE), jnp.int32),
+            pltpu.VMEM((PAIRS, K, 2 * TILE), F32),
+            pltpu.VMEM((NB, TILE, TILE), F32),
+            pltpu.VMEM((K, K), F32),
+            pltpu.VMEM((K, K), F32),
+            pltpu.VMEM((K, K), F32),
+            pltpu.VMEM((K, K), F32),
+            pltpu.VMEM((2, PLANE, PART, K), F32),
+            pltpu.VMEM((2, NODE * CORES, PART, K), F32),
+            pltpu.VMEM((STEPS, K, SPAN), BF16),
+            pltpu.VMEM((STEPS, K, SPAN), BF16),
+            pltpu.VMEM((STEPS, K, SPAN), F32),
+            pltpu.VMEM((K, K), F32),
+            pltpu.SemaphoreType.DMA((2, 3, 2, PLANE)),
+            pltpu.SemaphoreType.DMA((2, NODE)),
+            pltpu.SemaphoreType.DMA((2, WIDE)),
+            pltpu.SemaphoreType.DMA((2, WIDE)),
+            pltpu.SemaphoreType.DMA((2, 2, 2, 8)),
             pltpu.SemaphoreType.DMA((2, 2, 2, 2)),
             pltpu.SemaphoreType.DMA((2, 2, SIDE, 2, 2)),
             pltpu.SemaphoreType.DMA((2, 2, PLANE)),
+            pltpu.SemaphoreType.DMA((TILES,)),
+            pltpu.SemaphoreType.DMA((2,)),
+            pltpu.SemaphoreType.DMA((2,)),
             pltpu.SemaphoreType.DMA,
         ],
-        compiler_params=pltpu.CompilerParams(collective_id=1, has_side_effects=True),
-        name="deliver",
-    )(users, partial)
+        compiler_params=pltpu.CompilerParams(
+            collective_id=0, has_side_effects=True, vmem_limit_bytes=60 * 1024 * 1024
+        ),
+        name="step",
+    )(item, req, place, where, weights, user)
 
 
 def mask_kernel(table, boxes, out):
@@ -576,9 +565,9 @@
 
 def body(item_factors, need_owner, need_slot, block_index, block_count, weights, user_old):
     req, place, where = plan(need_owner[:, 0], need_slot, block_index, block_count)
-    lists, gram, table = fetch(item_factors.T, req.reshape(1, TILE), place)
-    users_new, partial = solve(lists, weights, user_old, gram, where)
-    boxes, user_gram = deliver(users_new, partial)
+    users_new, user_gram, boxes, table = step(
+        item_factors.T, req.reshape(1, TILE), place, where, weights, user_old
+    )
     return users_new, user_gram, mask(table, boxes)
 
 

time: 189 us -> 159 us (0.84)
  Pallas kernels: 179 us -> 156 us
  local copies, waits for them, and re-layouts: 8.68 us -> 1.41 us
    pallas_call x3 -> x1, Pallas kernels: 167 us -> 144 us  [step(): pl.pallas_call(step_kernel, out_shape=[jax.ShapeDtypeStruct((K, K), F32),...]
    unnamed x19 -> x6, local copies, waits for them, and re-layouts: 8.68 us -> 1.41 us
where the time goes in v2:
time: 159 us
  Pallas kernels  156 us (98%)
    pallas_call x1, Pallas kernels, step(): pl.pallas_call(step_kernel, out_shape=[jax.ShapeDtypeStruct((K, K), F32),...  144 us
    pallas_call x1, Pallas kernels, mask(): pl.pallas_call(mask_kernel, grid=(WIDE // 4,), out_shape=jax.ShapeDtypeSt...  9.34 us

profile of v2, /device:TPU:1, one launch (start us, length us, event | category | flops | bytes accessed | tf_op | source)
XLA Modules:
  0.0 158.6 jit_solution(17826204216743133568)
XLA Ops:
  1.3 2.8 %plan.1 = (s32[128]{0:T(128)}, s32[32]{0:T(128)}, s32[64]{0:T(128)}) custom-call(s32[32]{0:T(128)} %bitcast.5, s32[32]{0:T(128)} %slot.1, s32[64]{0:T(128)} %index.1, s32[1]{0:T(128)S(6)} %copy.12.count), custom_call_target="tpu_custom_call" | custom-call | tf_op jit(solution)/shard_map/plan/pallas_call | solution.py:166
  4.1 143.7 %step.1 = (f32[256,256]{1,0:T(8,128)}, f32[256,256]{1,0:T(8,128)}, f32[32,256,256]{2,1,0:T(8,128)}, s32[32,1,128]{2,1,0:T(1,128)}) custom-call(f32[64,8192]{1,0:T(8,128)} %bitcast.3, s32[1,128]{1,0:T(1,128)} %bitcast.4, s32[32]{0:T(128)} %get-tuple-element.11.place, s32[64]{0:T(128)} %get-tuple-element.12.where, f32[64,128,128]{2,1,0:T(8,128)} %weights_in.1, ...), custom_call_target="tpu_custom_call" | custom-call | tf_op jit(solution)/shard_map/step/pallas_call | solution.py:500
  147.8 0.0 copy-start.1
  147.8 0.0 copy-start
  147.9 9.3 %mask.1 = f32[1,32,256,256]{3,2,1,0:T(8,128)} custom-call(s32[32,1,128]{2,1,0:T(1,128)} %get-tuple-element.15.table, f32[32,256,256]{2,1,0:T(8,128)} %get-tuple-element.16.boxes), custom_call_target="tpu_custom_call" | custom-call | tf_op jit(solution)/shard_map/mask/pallas_call | solution.py:556
  157.2 0.0 copy-done.1
  157.2 0.7 copy.13
  157.9 0.0 copy-done
  157.9 0.7 copy.14
Async XLA Ops:
  147.8 9.4 %copy-start.1 = (f32[256,256]{1,0:T(8,128)S(1)}, f32[256,256]{1,0:T(8,128)}, u32[]{:S(2)}) copy-start(f32[256,256]{1,0:T(8,128)} %get-tuple-element.20) | copy-start | bytes 786436
  147.8 10.1 %copy-start = (f32[256,256]{1,0:T(8,128)S(1)}, f32[256,256]{1,0:T(8,128)}, u32[]{:S(2)}) copy-start(f32[256,256]{1,0:T(8,128)} %get-tuple-element.21) | copy-start | bytes 786436

commit v3 on v2

--- a/solution.py
+++ b/solution.py
@@ -12,6 +12,7 @@
 NEED = 32
 K = 256
 QUARTER = 64
+RANKS = QUARTER // 2
 NB = 64
 WIDE = 32
 NODE = 4
@@ -180,11 +181,12 @@
 def step_kernel(
     item, req, place, where, weights_in, user_in,
     users_new, user_gram, boxes, table,
-    tiles, full, outbox, inbox, asked, lists, weights, user, users, gram, part, red, mid, high, low, dense, spread,
+    tiles, full, relay, outbox, inbox_low, inbox_high, asked, lists, weights, user, users, gram, part, red, mid, high, low, dense, spread,
     sum_sems, row_sems, ask_sems, tile_sems, ring_sems, line_sems, cross_sems, sib_sems,
     load_sems, bring_sems, own_sems, local_sem,
 ):
     wide, node, spot, core = place_at()
+    inboxes = inbox_low, inbox_high
 
     def load(t):
         return pltpu.make_async_copy(
@@ -204,10 +206,28 @@
     def share(x):
         return pl.ds(pl.multiple_of(x * SHARE, SHARE), SHARE)
 
-    def rows_to(dx):
-        x = lax.rem(node + dx, NODE)
-        return remote(
-            tiles.at[share(x)], full.at[:, quarter(node), :], row_sems.at[0, dx], row_sems.at[1, dx], wide, x
+    right, left = lax.rem(node + 1, NODE), lax.rem(node + NODE - 1, NODE)
+    across = lax.rem(node + 2, NODE)
+
+    def part_share(x, way):
+        return pl.ds(pl.multiple_of(x * SHARE + way * SHARE // 2, SHARE // 2), SHARE // 2)
+
+    def rows_near(way):
+        x = (right, left)[way]
+        return remote(
+            tiles.at[share(x)], full.at[:, quarter(node), :], row_sems.at[0, 0, way], row_sems.at[1, 0, way], wide, x
+        )
+
+    def rows_relay(way):
+        return remote(
+            tiles.at[part_share(across, way)], relay.at[way],
+            row_sems.at[0, 1, way], row_sems.at[1, 1, way], wide, (right, left)[way],
+        )
+
+    def rows_far(way):
+        return remote(
+            relay.at[way], full.at[pl.ds(way * SHARE // 2, SHARE // 2), quarter((left, right)[way]), :],
+            row_sems.at[0, 2, way], row_sems.at[1, 2, way], wide, (right, left)[way],
         )
 
     def ask(k):
@@ -215,16 +235,19 @@
             req, table.at[wide], ask_sems.at[0, k], ask_sems.at[1, k], lax.rem(wide + k, WIDE), node
         )
 
-    def serve(k):
+    def serve(k, part):
         other = lax.rem(wide + k, WIDE)
         return remote(
-            outbox.at[other], inbox.at[pl.ds(2 * wide, 2)], tile_sems.at[0, k], tile_sems.at[1, k], other, node
+            outbox.at[part, other], inboxes[part].at[pl.ds(2 * wide, 2)],
+            tile_sems.at[0, part, k], tile_sems.at[1, part, k], other, node,
         )
 
     each(1, WIDE, lambda k: ask(k).start())
     each(0, TILES, lambda t: load(t).wait())
-    for dx in (1, 3, 2):
-        rows_to(dx).start()
+    for way in range(2):
+        rows_relay(way).start()
+    for way in range(2):
+        rows_near(way).start()
     table[wide] = req[...]
     full[:, quarter(node), :] = tiles[share(node)]
     each(1, WIDE, lambda k: ask(k).wait_recv())
@@ -232,21 +255,50 @@
     to_scalars.start()
     to_scalars.wait()
 
-    def tile(other, r):
-        return tiles[jnp.maximum(asked[other, 0, 2 * wide + r], 0)]
-
-    def fill(k):
+    def fill(k, part):
         other = lax.rem(wide + k, WIDE)
         for r in range(2):
-            outbox[other, r] = tile(other, r)
-        serve(k).start()
-
-    each(1, WIDE, fill)
+            at = jnp.maximum(asked[other, 0, 2 * wide + r], 0)
+            outbox[part, other, r] = tiles[at, part * RANKS : (part + 1) * RANKS, :]
+        serve(k, part).start()
+
+    for part_rank in range(2):
+        each(1, WIDE, lambda k, part_rank=part_rank: fill(k, part_rank))
     for r in range(2):
-        inbox[2 * wide + r] = tile(wide, r)
-
-    for dx in (1, 3, 2):
-        rows_to(dx).wait_recv()
+        mine = tiles[jnp.maximum(asked[wide, 0, 2 * wide + r], 0)]
+        for half in range(2):
+            inboxes[half][2 * wide + r] = mine[half * RANKS : (half + 1) * RANKS]
+    for way in range(2):
+        rows_relay(way).wait_recv()
+        rows_far(way).start()
+
+    def pass_on(c, x, way, half):
+        stage = 0 if x is node else 1
+        ranks = pl.ds(pl.multiple_of(x * QUARTER + half * RANKS, RANKS), RANKS)
+        here = lists.at[pl.ds(GROUP * c, GROUP), ranks, :]
+        sems = ring_sems.at[half, stage]
+        return remote(here, here, sems.at[0, way, c], sems.at[1, way, c], wide, (right, left)[way])
+
+    def pick(c, half):
+        ranks = pl.ds(pl.multiple_of(node * QUARTER + half * RANKS, RANKS), RANKS)
+        for j in range(GROUP):
+            for r in range(2):
+                at = place[2 * GROUP * c + 2 * j + r]
+                lists[GROUP * c + j, ranks, r * TILE : (r + 1) * TILE] = inboxes[half][at]
+        pass_on(c, node, 0, half).start()
+        pass_on(c, node, 1, half).start()
+
+    def forward(c, half):
+        pass_on(2 * c, node, 0, half).wait_recv()
+        pass_on(2 * c, left, 0, half).start()
+        pass_on(2 * c + 1, node, 1, half).wait_recv()
+        pass_on(2 * c + 1, right, 1, half).start()
+
+    each(1, WIDE, lambda k: serve(k, 0).wait_recv())
+    each(0, STEPS, lambda c: pick(c, 0))
+    for way in range(2):
+        rows_near(way).wait_recv()
+        rows_far(way).wait_recv()
     part[...] = jnp.zeros_like(part)
 
     def multiply(i):
@@ -257,37 +309,13 @@
     summer = Summer(part, gram, red.at[0], mid.at[0], sum_sems.at[0])
     summer.first()
 
-    each(1, WIDE, lambda k: serve(k).wait_recv())
-
-    right, left = lax.rem(node + 1, NODE), lax.rem(node + NODE - 1, NODE)
-
-    def pass_on(c, x, way):
-        own = x is node
-        stage = 0 if own else 1
-        here = lists.at[pl.ds(2 * c, 2), quarter(x), :]
-        return remote(
-            here, here, ring_sems.at[stage, 0, way, c], ring_sems.at[stage, 1, way, c], wide, (right, left)[way]
-        )
-
-    def pick(c):
-        for j in range(2):
-            for r in range(2):
-                lists[2 * c + j, quarter(node), r * TILE : (r + 1) * TILE] = inbox[place[4 * c + 2 * j + r]]
-        pass_on(c, node, 0).start()
-        pass_on(c, node, 1).start()
-
-    each(0, 8, pick)
+    each(0, STEPS // 2, lambda c: forward(c, 0))
+    each(1, WIDE, lambda k: serve(k, 1).wait_recv())
+    each(0, STEPS, lambda c: pick(c, 1))
     summer.second()
-
-    def forward(c):
-        pass_on(2 * c, node, 0).wait_recv()
-        pass_on(2 * c, left, 0).start()
-        pass_on(2 * c + 1, node, 1).wait_recv()
-        pass_on(2 * c + 1, right, 1).start()
-
-    each(0, 2, forward)
+    forward(0, 1)
     summer.third()
-    each(2, 4, forward)
+    forward(1, 1)
     bring_weights.wait()
     bring_user.wait()
 
@@ -295,14 +323,15 @@
     pair = split(x)
     spread[...] = jnp.zeros_like(spread)
 
-    def arrive(c):
-        pass_on(2 * c, node, 1).wait_recv()
-        pass_on(2 * c + 1, node, 0).wait_recv()
-        pass_on(2 * c, left, 0).wait_recv()
-        pass_on(2 * c + 1, right, 1).wait_recv()
+    def arrive(c, half):
+        pass_on(2 * c, node, 1, half).wait_recv()
+        pass_on(2 * c + 1, node, 0, half).wait_recv()
+        pass_on(2 * c, left, 0, half).wait_recv()
+        pass_on(2 * c + 1, right, 1, half).wait_recv()
+
+    each(0, STEPS // 2, lambda c: arrive(c, 0))
 
     def begin(i):
-        arrive(i)
         parts = [split(lists[GROUP * i + j]) for j in range(GROUP)]
         v = tuple(jnp.concatenate([q[k] for q in parts], axis=1) for k in range(2))
         high[i], low[i] = v
@@ -320,7 +349,9 @@
             rows.append(jnp.concatenate(cols, axis=1))
         spread[...] += dot3(split(jnp.concatenate(rows, axis=0)), v, (1, 1))
 
-    each(0, STEPS, begin)
+    for c in range(STEPS // 2):
+        arrive(c, 1)
+        each(2 * c, 2 * c + 2, begin)
     summer.last()
 
     gram_pair = split(gram[...])
@@ -476,21 +507,19 @@
     own.wait()
     give.wait()
 
-    def drain(c):
-        pass_on(c, node, 0).wait_send()
-        pass_on(c, node, 1).wait_send()
-
-    each(0, 8, drain)
-
-    def drain_far(c):
-        pass_on(2 * c, left, 0).wait_send()
-        pass_on(2 * c + 1, right, 1).wait_send()
-
-    each(0, 4, drain_far)
-    for dx in (1, 3, 2):
-        rows_to(dx).wait_send()
+    for half in range(2):
+        for way in range(2):
+            each(0, STEPS, lambda c, half=half, way=way: pass_on(c, node, way, half).wait_send())
+        for c in range(STEPS // 2):
+            pass_on(2 * c, left, 0, half).wait_send()
+            pass_on(2 * c + 1, right, 1, half).wait_send()
+    for way in range(2):
+        rows_relay(way).wait_send()
+        rows_near(way).wait_send()
+        rows_far(way).wait_send()
     each(1, WIDE, lambda k: ask(k).wait_send())
-    each(1, WIDE, lambda k: serve(k).wait_send())
+    for part_rank in range(2):
+        each(1, WIDE, lambda k, part_rank=part_rank: serve(k, part_rank).wait_send())
 
 
 def step(item, req, place, where, weights, user):
@@ -502,16 +531,18 @@
         out_shape=[
             jax.ShapeDtypeStruct((K, K), F32),
             jax.ShapeDtypeStruct((K, K), F32),
-            jax.ShapeDtypeStruct((WIDE, K, K), F32),
+            pltpu.VMEM((WIDE, K, K), F32),
             jax.ShapeDtypeStruct((WIDE, 1, TILE), jnp.int32),
         ],
         in_specs=[hbm, vmem, smem, smem, hbm, hbm],
-        out_specs=[hbm, vmem, hbm, vmem],
+        out_specs=[hbm, vmem, vmem, vmem],
         scratch_shapes=[
             pltpu.VMEM((TILES, QUARTER, TILE), F32),
             pltpu.VMEM((SHARE, K, TILE), F32),
-            pltpu.VMEM((WIDE, 2, QUARTER, TILE), F32),
-            pltpu.VMEM((2 * WIDE, QUARTER, TILE), F32),
+            pltpu.VMEM((2, SHARE // 2, QUARTER, TILE), F32),
+            pltpu.VMEM((2, WIDE, 2, RANKS, TILE), F32),
+            pltpu.VMEM((2 * WIDE, RANKS, TILE), F32),
+            pltpu.VMEM((2 * WIDE, RANKS, TILE), F32),
             pltpu.SMEM((WIDE, 1, TILE), jnp.int32),
             pltpu.VMEM((PAIRS, K, 2 * TILE), F32),
             pltpu.VMEM((NB, TILE, TILE), F32),
@@ -526,10 +557,10 @@
             pltpu.VMEM((STEPS, K, SPAN), F32),
             pltpu.VMEM((K, K), F32),
             pltpu.SemaphoreType.DMA((2, 3, 2, PLANE)),
-            pltpu.SemaphoreType.DMA((2, NODE)),
+            pltpu.SemaphoreType.DMA((2, 3, 2)),
             pltpu.SemaphoreType.DMA((2, WIDE)),
-            pltpu.SemaphoreType.DMA((2, WIDE)),
-            pltpu.SemaphoreType.DMA((2, 2, 2, 8)),
+            pltpu.SemaphoreType.DMA((2, 2, WIDE)),
+            pltpu.SemaphoreType.DMA((2, 2, 2, 2, STEPS)),
             pltpu.SemaphoreType.DMA((2, 2, 2, 2)),
             pltpu.SemaphoreType.DMA((2, 2, SIDE, 2, 2)),
             pltpu.SemaphoreType.DMA((2, 2, PLANE)),
@@ -539,26 +570,39 @@
             pltpu.SemaphoreType.DMA,
         ],
         compiler_params=pltpu.CompilerParams(
-            collective_id=0, has_side_effects=True, vmem_limit_bytes=60 * 1024 * 1024
+            collective_id=0, has_side_effects=True, vmem_limit_bytes=50 * 1024 * 1024
         ),
         name="step",
     )(item, req, place, where, weights, user)
 
 
-def mask_kernel(table, boxes, out):
+def mask_kernel(table, boxes, out, zeros, sems):
     wide = lax.axis_index("wide")
-    for j in range(4):
-        named = table[pl.program_id(0) * 4 + j, 0, 2 * wide] >= 0
-        out[0, j] = jnp.where(named, boxes[j], 0.0)
+    zeros[...] = jnp.zeros_like(zeros)
+
+    def begin(g):
+        named = table[g, 0, 2 * wide] >= 0
+
+        @pl.when(named)
+        def _():
+            pltpu.make_async_copy(boxes.at[g], out.at[0, g], sems.at[g]).start()
+
+        @pl.when(jnp.logical_not(named))
+        def _():
+            pltpu.make_async_copy(zeros, out.at[0, g], sems.at[g]).start()
+
+    each(0, WIDE, begin)
+    each(0, WIDE, lambda g: pltpu.make_async_copy(zeros, out.at[0, g], sems.at[g]).wait())
 
 
 def mask(table, boxes):
     return pl.pallas_call(
         mask_kernel,
-        grid=(WIDE // 4,),
         out_shape=jax.ShapeDtypeStruct((1, WIDE, K, K), F32),
-        in_specs=[pl.BlockSpec(memory_space=pltpu.SMEM), pl.BlockSpec((4, K, K), lambda g: (g, 0, 0))],
-        out_specs=pl.BlockSpec((1, 4, K, K), lambda g: (0, g, 0, 0)),
+        in_specs=[pl.BlockSpec(memory_space=pltpu.SMEM), pl.BlockSpec(memory_space=pltpu.VMEM)],
+        out_specs=pl.BlockSpec(memory_space=pl.ANY),
+        scratch_shapes=[pltpu.VMEM((K, K), F32), pltpu.SemaphoreType.DMA((WIDE,))],
+        compiler_params=pltpu.CompilerParams(vmem_limit_bytes=10 * 1024 * 1024),
         name="mask",
     )(table, boxes)
 

time: 159 us -> 144 us (0.906)
  Pallas kernels: 156 us -> 141 us
    pallas_call x1, Pallas kernels: 144 us -> 133 us  [step(): pl.pallas_call(step_kernel, out_shape=[jax.ShapeDtypeStruct((K, K), F32),...]
    pallas_call x1, Pallas kernels: 9.34 us -> 4.36 us  [mask(): pl.pallas_call(mask_kernel, out_shape=jax.ShapeDtypeStruct((1, WIDE, K, K...]
where the time goes in v3:
time: 144 us
  Pallas kernels  141 us (98%)
  local copies, waits for them, and re-layouts  2.13 us (1%)
    pallas_call x1, Pallas kernels, step(): pl.pallas_call(step_kernel, out_shape=[jax.ShapeDtypeStruct((K, K), F32),...  133 us
    pallas_call x1, Pallas kernels, mask(): pl.pallas_call(mask_kernel, out_shape=jax.ShapeDtypeStruct((1, WIDE, K, K...  4.36 us

profile of v3, /device:TPU:1, one launch (start us, length us, event | category | flops | bytes accessed | tf_op | source)
XLA Modules:
  0.0 144.0 jit_solution(6473570511895263636)
XLA Ops:
  1.3 2.9 %plan.1 = (s32[128]{0:T(128)}, s32[32]{0:T(128)}, s32[64]{0:T(128)}) custom-call(s32[32]{0:T(128)} %bitcast.5, s32[32]{0:T(128)} %slot.1, s32[64]{0:T(128)} %index.1, s32[1]{0:T(128)S(6)} %copy.12.count), custom_call_target="tpu_custom_call" | custom-call | tf_op jit(solution)/shard_map/plan/pallas_call | solution.py:167
  4.1 133.3 %step.1 = (f32[256,256]{1,0:T(8,128)}, f32[256,256]{1,0:T(8,128)}, f32[32,256,256]{2,1,0:T(8,128)S(1)}, s32[32,1,128]{2,1,0:T(1,128)}) custom-call(f32[64,8192]{1,0:T(8,128)} %bitcast.3, s32[1,128]{1,0:T(1,128)} %bitcast.4, s32[32]{0:T(128)} %get-tuple-element.11.place, s32[64]{0:T(128)} %get-tuple-element.12.where, f32[64,128,128]{2,1,0:T(8,128)} %weights_in.1, ...), custom_call_target="tpu_custom_call" | custom-call | tf_op jit(solution)/shard_map/step/pallas_call | solution.py:529
  137.5 0.0 copy-start
  137.5 0.7 copy-done
  138.2 0.0 copy-start.2
  138.2 0.0 copy-start.1
  138.2 4.4 %mask.1 = f32[1,32,256,256]{3,2,1,0:T(8,128)} custom-call(s32[32,1,128]{2,1,0:T(1,128)S(1)} %copy-done, f32[32,256,256]{2,1,0:T(8,128)S(1)} %get-tuple-element.16.boxes), custom_call_target="tpu_custom_call" | custom-call | tf_op jit(solution)/shard_map/mask/pallas_call | solution.py:599
  142.6 0.0 copy-done.2
  142.6 0.7 copy.13
  143.3 0.0 copy-done.1
  143.3 0.7 copy.14
Async XLA Ops:
  137.5 0.7 copy-start
  138.2 4.4 %copy-start.2 = (f32[256,256]{1,0:T(8,128)S(1)}, f32[256,256]{1,0:T(8,128)}, u32[]{:S(2)}) copy-start(f32[256,256]{1,0:T(8,128)} %get-tuple-element.20) | copy-start | bytes 786436
  138.2 5.1 %copy-start.1 = (f32[256,256]{1,0:T(8,128)S(1)}, f32[256,256]{1,0:T(8,128)}, u32[]{:S(2)}) copy-start(f32[256,256]{1,0:T(8,128)} %get-tuple-element.21) | copy-start | bytes 786436

commit v4 on v3

--- a/solution.py
+++ b/solution.py
@@ -27,6 +27,8 @@
 SPAN = GROUP * 2 * TILE
 HALF = 128
 BIT = 64
+BAND = K // (NODE * CORES)
+STRIP = BAND // SIDE
 PART = K // PLANE
 RIDGE = 1.0
 EPS = 1e-06
@@ -133,6 +135,82 @@
         each(1, PLANE, lambda k: self.over_plane(k, 0).wait_send())
         each(1, NODE * CORES, lambda k: self.over_eight(k).wait_send())
         each(1, PLANE, lambda k: self.over_plane(k, 2).wait_send())
+
+
+class LineSummer:
+    def __init__(self, part, total, eight, own, along_y, along_z, sems):
+        self.part, self.total, self.eight, self.own = part, total, eight, own
+        self.along_y, self.along_z, self.sems = along_y, along_z, sems
+        self.wide, self.node, self.spot, self.core = place_at()
+        self.y, self.z = self.spot // SIDE, lax.rem(self.spot, SIDE)
+        self.eighth = self.node * CORES + self.core
+
+    def rows(self, eighth):
+        return pl.ds(pl.multiple_of(eighth * BAND, BAND), BAND)
+
+    def over_eight(self, k, stage):
+        other = lax.rem(self.eighth + k, NODE * CORES)
+        if stage == 0:
+            src, dst = self.part.at[self.rows(other)], self.eight.at[self.eighth]
+        else:
+            src = dst = self.total.at[self.rows(self.eighth)]
+        wide = self.spot * CORES + lax.rem(other, CORES)
+        return remote(src, dst, self.sems.at[stage, 0, k], self.sems.at[stage, 1, k], wide, other // CORES)
+
+    def over_y(self, k, stage):
+        other = lax.rem(self.y + k, SIDE)
+        if stage == 1:
+            src, dst = self.own.at[other], self.along_y.at[self.y]
+        else:
+            src = dst = self.total.at[self.fine()]
+        wide = (other * SIDE + self.z) * CORES + self.core
+        return remote(src, dst, self.sems.at[stage, 0, k], self.sems.at[stage, 1, k], wide, self.node)
+
+    def over_z(self, k):
+        wide = (self.y * SIDE + lax.rem(self.z + k, SIDE)) * CORES + self.core
+        slot = self.along_z.at[self.z]
+        return remote(slot, slot, self.sems.at[2, 0, k], self.sems.at[2, 1, k], wide, self.node)
+
+    def fine(self):
+        return pl.ds(pl.multiple_of(self.eighth * BAND + self.y * STRIP, STRIP), STRIP)
+
+    def first(self):
+        each(1, NODE * CORES, lambda k: self.over_eight(k, 0).start())
+        self.eight[self.eighth] = self.part[self.rows(self.eighth), :]
+
+    def second(self):
+        each(1, NODE * CORES, lambda k: self.over_eight(k, 0).wait_recv())
+        for j in range(SIDE):
+            rows = slice(j * STRIP, (j + 1) * STRIP)
+            total = self.eight[0, rows, :]
+            for i in range(1, NODE * CORES):
+                total = total + self.eight[i, rows, :]
+            self.own[j] = total
+        each(1, SIDE, lambda k: self.over_y(k, 1).start())
+        self.along_y[self.y] = self.own[self.y]
+
+    def third(self):
+        each(1, SIDE, lambda k: self.over_y(k, 1).wait_recv())
+        self.along_z[self.z] = (self.along_y[0] + self.along_y[1]) + (self.along_y[2] + self.along_y[3])
+        each(1, SIDE, lambda k: self.over_z(k).start())
+
+    def fourth(self):
+        each(1, SIDE, lambda k: self.over_z(k).wait_recv())
+        total = (self.along_z[0] + self.along_z[1]) + (self.along_z[2] + self.along_z[3])
+        self.total[self.fine(), :] = total
+        each(1, SIDE, lambda k: self.over_y(k, 3).start())
+
+    def fifth(self):
+        each(1, SIDE, lambda k: self.over_y(k, 3).wait_recv())
+        each(1, NODE * CORES, lambda k: self.over_eight(k, 4).start())
+
+    def last(self):
+        each(1, NODE * CORES, lambda k: self.over_eight(k, 4).wait_recv())
+        each(1, NODE * CORES, lambda k: self.over_eight(k, 0).wait_send())
+        each(1, SIDE, lambda k: self.over_y(k, 1).wait_send())
+        each(1, SIDE, lambda k: self.over_z(k).wait_send())
+        each(1, SIDE, lambda k: self.over_y(k, 3).wait_send())
+        each(1, NODE * CORES, lambda k: self.over_eight(k, 4).wait_send())
 
 
 def plan_kernel(owner, slot, index, count, req, place, where, seen):
@@ -180,9 +258,9 @@
 
 def step_kernel(
     item, req, place, where, weights_in, user_in,
-    users_new, user_gram, boxes, table,
-    tiles, full, relay, outbox, inbox_low, inbox_high, asked, lists, weights, user, users, gram, part, red, mid, high, low, dense, spread,
-    sum_sems, row_sems, ask_sems, tile_sems, ring_sems, line_sems, cross_sems, sib_sems,
+    users, user_gram, boxes, table,
+    tiles, full, relay, outbox, inbox_low, inbox_high, asked, lists, weights, user, gram, part, red, mid, eight, own_band, along_y, along_z, high, low, dense, spread,
+    sum_sems, line_sum_sems, row_sems, ask_sems, tile_sems, ring_sems, line_sems, cross_sems, sib_sems,
     load_sems, bring_sems, own_sems, local_sem,
 ):
     wide, node, spot, core = place_at()
@@ -306,16 +384,15 @@
         part[...] += dot3(pair, pair, (1, 1))
 
     each(0, SHARE // 4, multiply)
-    summer = Summer(part, gram, red.at[0], mid.at[0], sum_sems.at[0])
+    summer = Summer(part, gram, red, mid, sum_sems)
     summer.first()
 
     each(0, STEPS // 2, lambda c: forward(c, 0))
     each(1, WIDE, lambda k: serve(k, 1).wait_recv())
+    summer.second()
     each(0, STEPS, lambda c: pick(c, 1))
-    summer.second()
-    forward(0, 1)
+    each(0, STEPS // 2, lambda c: forward(c, 1))
     summer.third()
-    forward(1, 1)
     bring_weights.wait()
     bring_user.wait()
 
@@ -447,8 +524,6 @@
 
     own = pltpu.make_async_copy(users, boxes.at[wide], own_sems.at[0])
     own.start()
-    give = pltpu.make_async_copy(users, users_new, own_sems.at[1])
-    give.start()
     for half in range(2):
         for way in range(2):
             line(half, way, 0).start()
@@ -460,7 +535,7 @@
 
     pair = split(x)
     part[...] = dot3(pair, pair, (0, 0))
-    summer = Summer(part, user_gram, red.at[1], mid.at[1], sum_sems.at[1])
+    summer = LineSummer(part, user_gram, eight, own_band, along_y, along_z, line_sum_sems)
     summer.first()
 
     def come_from(way):
@@ -487,12 +562,16 @@
                 cross(half, along, way, 0).wait_recv()
                 cross(half, along, way, 1).start()
                 sibling(half, along, come_from(way)).start()
-    summer.last()
+        if along == -1:
+            summer.fourth()
+        if along == 2:
+            summer.fifth()
     for along in (0, -1, 1, 2):
         for half in range(2):
             for way in range(2):
                 cross(half, along, way, 1).wait_recv()
             sibling(half, along, 2).start()
+    summer.last()
     for along in (0, -1, 1, 2):
         for half in range(2):
             for over in (0, -1, 1, 2):
@@ -505,7 +584,6 @@
             for far in range(2):
                 line(half, way, far).wait_send()
     own.wait()
-    give.wait()
 
     for half in range(2):
         for way in range(2):
@@ -529,13 +607,13 @@
     return pl.pallas_call(
         step_kernel,
         out_shape=[
-            jax.ShapeDtypeStruct((K, K), F32),
-            jax.ShapeDtypeStruct((K, K), F32),
+            pltpu.VMEM((K, K), F32),
+            pltpu.VMEM((K, K), F32),
             pltpu.VMEM((WIDE, K, K), F32),
-            jax.ShapeDtypeStruct((WIDE, 1, TILE), jnp.int32),
+            pltpu.VMEM((WIDE, 1, TILE), jnp.int32),
         ],
         in_specs=[hbm, vmem, smem, smem, hbm, hbm],
-        out_specs=[hbm, vmem, vmem, vmem],
+        out_specs=[vmem] * 4,
         scratch_shapes=[
             pltpu.VMEM((TILES, QUARTER, TILE), F32),
             pltpu.VMEM((SHARE, K, TILE), F32),
@@ -549,14 +627,18 @@
             pltpu.VMEM((K, K), F32),
             pltpu.VMEM((K, K), F32),
             pltpu.VMEM((K, K), F32),
-            pltpu.VMEM((K, K), F32),
-            pltpu.VMEM((2, PLANE, PART, K), F32),
-            pltpu.VMEM((2, NODE * CORES, PART, K), F32),
+            pltpu.VMEM((PLANE, PART, K), F32),
+            pltpu.VMEM((NODE * CORES, PART, K), F32),
+            pltpu.VMEM((NODE * CORES, BAND, K), F32),
+            pltpu.VMEM((SIDE, STRIP, K), F32),
+            pltpu.VMEM((SIDE, STRIP, K), F32),
+            pltpu.VMEM((SIDE, STRIP, K), F32),
             pltpu.VMEM((STEPS, K, SPAN), BF16),
             pltpu.VMEM((STEPS, K, SPAN), BF16),
             pltpu.VMEM((STEPS, K, SPAN), F32),
             pltpu.VMEM((K, K), F32),
-            pltpu.SemaphoreType.DMA((2, 3, 2, PLANE)),
+            pltpu.SemaphoreType.DMA((3, 2, PLANE)),
+            pltpu.SemaphoreType.DMA((5, 2, NODE * CORES)),
             pltpu.SemaphoreType.DMA((2, 3, 2)),
             pltpu.SemaphoreType.DMA((2, WIDE)),
             pltpu.SemaphoreType.DMA((2, 2, WIDE)),
@@ -566,7 +648,7 @@
             pltpu.SemaphoreType.DMA((2, 2, PLANE)),
             pltpu.SemaphoreType.DMA((TILES,)),
             pltpu.SemaphoreType.DMA((2,)),
-            pltpu.SemaphoreType.DMA((2,)),
+            pltpu.SemaphoreType.DMA((1,)),
             pltpu.SemaphoreType.DMA,
         ],
         compiler_params=pltpu.CompilerParams(
@@ -576,9 +658,16 @@
     )(item, req, place, where, weights, user)
 
 
-def mask_kernel(table, boxes, out, zeros, sems):
+def mask_kernel(rows, boxes, users_in, gram_in, users_new, user_gram, out, table, zeros, sems):
+    scalars = pltpu.make_async_copy(rows, table, sems.at[WIDE + 2])
+    scalars.start()
+    users = pltpu.make_async_copy(users_in, users_new, sems.at[WIDE])
+    gram = pltpu.make_async_copy(gram_in, user_gram, sems.at[WIDE + 1])
+    users.start()
+    gram.start()
     wide = lax.axis_index("wide")
     zeros[...] = jnp.zeros_like(zeros)
+    scalars.wait()
 
     def begin(g):
         named = table[g, 0, 2 * wide] >= 0
@@ -593,18 +682,28 @@
 
     each(0, WIDE, begin)
     each(0, WIDE, lambda g: pltpu.make_async_copy(zeros, out.at[0, g], sems.at[g]).wait())
-
-
-def mask(table, boxes):
+    users.wait()
+    gram.wait()
+
+
+def mask(table, boxes, users, gram):
     return pl.pallas_call(
         mask_kernel,
-        out_shape=jax.ShapeDtypeStruct((1, WIDE, K, K), F32),
-        in_specs=[pl.BlockSpec(memory_space=pltpu.SMEM), pl.BlockSpec(memory_space=pltpu.VMEM)],
-        out_specs=pl.BlockSpec(memory_space=pl.ANY),
-        scratch_shapes=[pltpu.VMEM((K, K), F32), pltpu.SemaphoreType.DMA((WIDE,))],
+        out_shape=[
+            jax.ShapeDtypeStruct((K, K), F32),
+            jax.ShapeDtypeStruct((K, K), F32),
+            jax.ShapeDtypeStruct((1, WIDE, K, K), F32),
+        ],
+        in_specs=[pl.BlockSpec(memory_space=pltpu.VMEM)] * 4,
+        out_specs=[pl.BlockSpec(memory_space=pl.ANY)] * 3,
+        scratch_shapes=[
+            pltpu.SMEM((WIDE, 1, TILE), jnp.int32),
+            pltpu.VMEM((K, K), F32),
+            pltpu.SemaphoreType.DMA((WIDE + 3,)),
+        ],
         compiler_params=pltpu.CompilerParams(vmem_limit_bytes=10 * 1024 * 1024),
         name="mask",
-    )(table, boxes)
+    )(table, boxes, users, gram)
 
 
 def body(item_factors, need_owner, need_slot, block_index, block_count, weights, user_old):
@@ -612,7 +711,7 @@
     users_new, user_gram, boxes, table = step(
         item_factors.T, req.reshape(1, TILE), place, where, weights, user_old
     )
-    return users_new, user_gram, mask(table, boxes)
+    return tuple(mask(table, boxes, users_new, user_gram))
 
 
 def solution(mesh):

time: 144 us -> 139 us (0.965)
  Pallas kernels: 141 us -> 137 us
  local copies, waits for them, and re-layouts: 2.13 us -> 0 us
    pallas_call x2, Pallas kernels: 138 us -> 134 us  [the longest x1 130 us: step(): pl.pallas_call(step_kernel, out_shape=[pltpu.VMEM((K, K), F32), pltpu.VME...]
    unnamed x8 -> x0, local copies, waits for them, and re-layouts: 2.13 us -> none
where the time goes in v4:
time: 139 us; the launch traced here: 138 us
  Pallas kernels  137 us (99%)
    pallas_call x1, Pallas kernels, step(): pl.pallas_call(step_kernel, out_shape=[pltpu.VMEM((K, K), F32), pltpu.VME...  130 us
    pallas_call x1, Pallas kernels, mask(): pl.pallas_call(mask_kernel, out_shape=[jax.ShapeDtypeStruct((K, K), F32),...  4.38 us
    pallas_call x1, Pallas kernels, plan(): pl.pallas_call(plan_kernel, out_shape=[jax.ShapeDtypeStruct((TILE,), jnp....  2.91 us

profile of v4, /device:TPU:1, one launch (start us, length us, event | category | flops | bytes accessed | tf_op | source)
XLA Modules:
  0.0 138.5 jit_solution(5642409247737247339)
XLA Ops:
  1.3 2.9 %plan.1 = (s32[128]{0:T(128)}, s32[32]{0:T(128)}, s32[64]{0:T(128)}) custom-call(s32[32]{0:T(128)} %bitcast.5, s32[32]{0:T(128)} %slot.1, s32[64]{0:T(128)} %index.1, s32[1]{0:T(128)S(6)} %copy.10.count), custom_call_target="tpu_custom_call" | custom-call | tf_op jit(solution)/shard_map/plan/pallas_call | solution.py:245
  4.2 129.9 %step.1 = (f32[256,256]{1,0:T(8,128)S(1)}, f32[256,256]{1,0:T(8,128)S(1)}, f32[32,256,256]{2,1,0:T(8,128)S(1)}, s32[32,1,128]{2,1,0:T(1,128)S(1)}) custom-call(f32[64,8192]{1,0:T(8,128)} %bitcast.3, s32[1,128]{1,0:T(1,128)} %bitcast.4, s32[32]{0:T(128)} %get-tuple-element.11.place, s32[64]{0:T(128)} %get-tuple-element.12.where, f32[64,128,128]{2,1,0:T(8,128)} %weights_in.1, ...), custom_call_target="tpu_custom_call" | custom-call | tf_op jit(solution)/shard_map/step/pallas_call | solution.py:607
  134.1 4.4 %mask.1 = (f32[256,256]{1,0:T(8,128)}, f32[256,256]{1,0:T(8,128)}, f32[1,32,256,256]{3,2,1,0:T(8,128)}) custom-call(s32[32,1,128]{2,1,0:T(1,128)S(1)} %get-tuple-element.13.rows, f32[32,256,256]{2,1,0:T(8,128)S(1)} %get-tuple-element.14.boxes, f32[256,256]{1,0:T(8,128)S(1)} %get-tuple-element.15.users_in, f32[256,256]{1,0:T(8,128)S(1)} %get-tuple-element.16.gram_in), custom_call_target="tpu_custom_call" | custom-call | tf_op jit(solution)/shard_map/mask/pallas_call | solution.py:690

commit v5 on v4

--- a/solution.py
+++ b/solution.py
@@ -24,7 +24,6 @@
 PAIRS = NEED // 2
 GROUP = 4
 STEPS = PAIRS // GROUP
-SPAN = GROUP * 2 * TILE
 HALF = 128
 BIT = 64
 BAND = K // (NODE * CORES)
@@ -214,30 +213,19 @@
 
 
 def plan_kernel(owner, slot, index, count, req, place, where, seen):
-    def clear(i):
+    for i in range(TILE):
         req[i] = -1
-        where[i] = -1
-
-    def clear_rest(i):
-        req[i] = -1
-
-    each(0, NB, clear)
-    each(NB, TILE, clear_rest)
-    each(0, WIDE, lambda i: seen.__setitem__(i, 0))
-
-    def entry(e):
+    for i in range(WIDE):
+        seen[i] = 0
+    for e in range(NEED):
         o = owner[e]
-        at = 2 * o + seen[o]
-        seen[o] = seen[o] + 1
-        place[e] = at
-        req[at] = slot[e]
-
-    each(0, NEED, entry)
-
-    def block(b):
-        where[index[b]] = b
-
-    each(0, count[0], block)
+        before = seen[o]
+        seen[o] = before + 1
+        place[e] = 2 * o + before
+        req[2 * o + before] = slot[e]
+    live = count[0]
+    for b in range(NB):
+        where[index[b]] = jnp.where(b < live, b, -1)
 
 
 def plan(owner, slot, index, count):
@@ -259,7 +247,7 @@
 def step_kernel(
     item, req, place, where, weights_in, user_in,
     users, user_gram, boxes, table,
-    tiles, full, relay, outbox, inbox_low, inbox_high, asked, lists, weights, user, gram, part, red, mid, eight, own_band, along_y, along_z, high, low, dense, spread,
+    tiles, full, relay, outbox, inbox_low, inbox_high, asked, lists, weights, user, gram, part, red, mid, eight, own_band, along_y, along_z, high, low, dense,
     sum_sems, line_sum_sems, row_sems, ask_sems, tile_sems, ring_sems, line_sems, cross_sems, sib_sems,
     load_sems, bring_sems, own_sems, local_sem,
 ):
@@ -398,7 +386,6 @@
 
     x = user[...]
     pair = split(x)
-    spread[...] = jnp.zeros_like(spread)
 
     def arrive(c, half):
         pass_on(2 * c, node, 1, half).wait_recv()
@@ -408,27 +395,28 @@
 
     each(0, STEPS // 2, lambda c: arrive(c, 0))
 
-    def begin(i):
-        parts = [split(lists[GROUP * i + j]) for j in range(GROUP)]
-        v = tuple(jnp.concatenate([q[k] for q in parts], axis=1) for k in range(2))
-        high[i], low[i] = v
+    def begin(p, total):
+        v = split(lists[p])
+        high[p], low[p] = v
         s = dot3(pair, v, (1, 0))
         rows = []
         for u in range(2):
             cols = []
-            for r in range(2 * GROUP):
-                at = where[u * NEED + 2 * GROUP * i + r]
+            for r in range(2):
+                at = where[u * NEED + 2 * p + r]
                 live = (jnp.minimum(at, 0) + 1).astype(F32)
                 c = weights[jnp.maximum(at, 0)] * live
                 here = slice(u * TILE, (u + 1) * TILE), slice(r * TILE, (r + 1) * TILE)
-                dense[i, here[0], here[1]] = c
+                dense[p, here[0], here[1]] = c
                 cols.append((c + live) - c * s[here])
             rows.append(jnp.concatenate(cols, axis=1))
-        spread[...] += dot3(split(jnp.concatenate(rows, axis=0)), v, (1, 1))
-
+        return total + dot3(split(jnp.concatenate(rows, axis=0)), v, (1, 1))
+
+    total = jnp.zeros((K, K), F32)
     for c in range(STEPS // 2):
         arrive(c, 1)
-        each(2 * c, 2 * c + 2, begin)
+        for p in range(c * PAIRS // 2, (c + 1) * PAIRS // 2):
+            total = begin(p, total)
     summer.last()
 
     gram_pair = split(gram[...])
@@ -436,20 +424,21 @@
     def globally(d, pair):
         return dot3(pair, gram_pair, (1, 0)) + RIDGE * d
 
-    residual = spread[...] - globally(x, pair)
+    residual = total - globally(x, pair)
     direction = residual
     norm = jnp.sum(residual * residual, axis=1, keepdims=True)
 
     pair = split(direction)
-    spread[...] = jnp.zeros_like(spread)
-
-    def apply(i):
-        v = (high[i], low[i])
-        t = dot3(pair, v, (1, 0)) * dense[i]
-        spread[...] += dot3(split(t), v, (1, 1))
-
-    each(0, STEPS, apply)
-    applied = spread[...] + globally(direction, pair)
+
+    def scores(p):
+        return dot3(pair, (high[p], low[p]), (1, 0))
+
+    applied = globally(direction, pair)
+    s = scores(0)
+    for p in range(PAIRS):
+        following = scores(p + 1) if p + 1 < PAIRS else None
+        applied = applied + dot3(split(s * dense[p]), (high[p], low[p]), (1, 1))
+        s = following
     step = norm / (jnp.sum(direction * applied, axis=1, keepdims=True) + EPS)
     x = x + step * direction
     residual = residual - step * applied
@@ -458,18 +447,11 @@
     norm = following
 
     pair = split(direction)
-    spread[...] = direction * globally(direction, pair)
-
-    def curve(i):
-        s = dot3(pair, (high[i], low[i]), (1, 0))
-        bend = s * s * dense[i]
-        total = spread[...]
-        for j in range(GROUP):
-            total = total + bend[:, j * 2 * TILE : (j + 1) * 2 * TILE]
-        spread[...] = total
-
-    each(0, STEPS, curve)
-    step = norm / (jnp.sum(spread[...], axis=1, keepdims=True) + EPS)
+    bend = direction * globally(direction, pair)
+    for p in range(PAIRS):
+        s = scores(p)
+        bend = bend + s * s * dense[p]
+    step = norm / (jnp.sum(bend, axis=1, keepdims=True) + EPS)
     x = x + step * direction
     users[...] = x
 
@@ -633,10 +615,9 @@
             pltpu.VMEM((SIDE, STRIP, K), F32),
             pltpu.VMEM((SIDE, STRIP, K), F32),
             pltpu.VMEM((SIDE, STRIP, K), F32),
-            pltpu.VMEM((STEPS, K, SPAN), BF16),
-            pltpu.VMEM((STEPS, K, SPAN), BF16),
-            pltpu.VMEM((STEPS, K, SPAN), F32),
-            pltpu.VMEM((K, K), F32),
+            pltpu.VMEM((PAIRS, K, 2 * TILE), BF16),
+            pltpu.VMEM((PAIRS, K, 2 * TILE), BF16),
+            pltpu.VMEM((PAIRS, K, 2 * TILE), F32),
             pltpu.SemaphoreType.DMA((3, 2, PLANE)),
             pltpu.SemaphoreType.DMA((5, 2, NODE * CORES)),
             pltpu.SemaphoreType.DMA((2, 3, 2)),

time: 139 us -> 132 us (0.950)
  Pallas kernels: 137 us -> 130 us
    pallas_call x1, Pallas kernels: 130 us -> 125 us  [step(): pl.pallas_call(step_kernel, out_shape=[pltpu.VMEM((K, K), F32), pltpu.VME...]
    pallas_call x1, Pallas kernels: 2.91 us -> 1.5 us  [plan(): pl.pallas_call(plan_kernel, out_shape=[jax.ShapeDtypeStruct((TILE,), jnp....]
where the time goes in v5:
time: 132 us
  Pallas kernels  130 us (98%)
    pallas_call x1, Pallas kernels, step(): pl.pallas_call(step_kernel, out_shape=[pltpu.VMEM((K, K), F32), pltpu.VME...  125 us
    pallas_call x1, Pallas kernels, mask(): pl.pallas_call(mask_kernel, out_shape=[jax.ShapeDtypeStruct((K, K), F32),...  4.38 us

profile of v5, /device:TPU:1, one launch (start us, length us, event | category | flops | bytes accessed | tf_op | source)
XLA Modules:
  0.0 131.7 jit_solution(2151855713603580937)
XLA Ops:
  1.3 1.5 %plan.1 = (s32[128]{0:T(128)}, s32[32]{0:T(128)}, s32[64]{0:T(128)}) custom-call(s32[32]{0:T(128)} %bitcast.5, s32[32]{0:T(128)} %slot.1, s32[64]{0:T(128)} %index.1, s32[1]{0:T(128)S(6)} %copy.10.count), custom_call_target="tpu_custom_call" | custom-call | tf_op jit(solution)/shard_map/plan/pallas_call | solution.py:233
  2.8 124.6 %step.1 = (f32[256,256]{1,0:T(8,128)S(1)}, f32[256,256]{1,0:T(8,128)S(1)}, f32[32,256,256]{2,1,0:T(8,128)S(1)}, s32[32,1,128]{2,1,0:T(1,128)S(1)}) custom-call(f32[64,8192]{1,0:T(8,128)} %bitcast.3, s32[1,128]{1,0:T(1,128)} %bitcast.4, s32[32]{0:T(128)} %get-tuple-element.11.place, s32[64]{0:T(128)} %get-tuple-element.12.where, f32[64,128,128]{2,1,0:T(8,128)} %weights_in.1, ...), custom_call_target="tpu_custom_call" | custom-call | tf_op jit(solution)/shard_map/step/pallas_call | solution.py:589
  127.4 4.4 %mask.1 = (f32[256,256]{1,0:T(8,128)}, f32[256,256]{1,0:T(8,128)}, f32[1,32,256,256]{3,2,1,0:T(8,128)}) custom-call(s32[32,1,128]{2,1,0:T(1,128)S(1)} %get-tuple-element.13.rows, f32[32,256,256]{2,1,0:T(8,128)S(1)} %get-tuple-element.14.boxes, f32[256,256]{1,0:T(8,128)S(1)} %get-tuple-element.15.users_in, f32[256,256]{1,0:T(8,128)S(1)} %get-tuple-element.16.gram_in), custom_call_target="tpu_custom_call" | custom-call | tf_op jit(solution)/shard_map/mask/pallas_call | solution.py:671

commit v6 on v5

--- a/solution.py
+++ b/solution.py
@@ -27,7 +27,6 @@
 HALF = 128
 BIT = 64
 BAND = K // (NODE * CORES)
-STRIP = BAND // SIDE
 PART = K // PLANE
 RIDGE = 1.0
 EPS = 1e-06
@@ -137,8 +136,8 @@
 
 
 class LineSummer:
-    def __init__(self, part, total, eight, own, along_y, along_z, sems):
-        self.part, self.total, self.eight, self.own = part, total, eight, own
+    def __init__(self, part, total, eight, along_y, along_z, sems):
+        self.part, self.total, self.eight = part, total, eight
         self.along_y, self.along_z, self.sems = along_y, along_z, sems
         self.wide, self.node, self.spot, self.core = place_at()
         self.y, self.z = self.spot // SIDE, lax.rem(self.spot, SIDE)
@@ -156,60 +155,45 @@
         wide = self.spot * CORES + lax.rem(other, CORES)
         return remote(src, dst, self.sems.at[stage, 0, k], self.sems.at[stage, 1, k], wide, other // CORES)
 
-    def over_y(self, k, stage):
-        other = lax.rem(self.y + k, SIDE)
-        if stage == 1:
-            src, dst = self.own.at[other], self.along_y.at[self.y]
-        else:
-            src = dst = self.total.at[self.fine()]
-        wide = (other * SIDE + self.z) * CORES + self.core
-        return remote(src, dst, self.sems.at[stage, 0, k], self.sems.at[stage, 1, k], wide, self.node)
+    def over_y(self, k):
+        wide = (lax.rem(self.y + k, SIDE) * SIDE + self.z) * CORES + self.core
+        slot = self.along_y.at[self.y]
+        return remote(slot, slot, self.sems.at[1, 0, k], self.sems.at[1, 1, k], wide, self.node)
 
     def over_z(self, k):
         wide = (self.y * SIDE + lax.rem(self.z + k, SIDE)) * CORES + self.core
         slot = self.along_z.at[self.z]
         return remote(slot, slot, self.sems.at[2, 0, k], self.sems.at[2, 1, k], wide, self.node)
 
-    def fine(self):
-        return pl.ds(pl.multiple_of(self.eighth * BAND + self.y * STRIP, STRIP), STRIP)
-
     def first(self):
         each(1, NODE * CORES, lambda k: self.over_eight(k, 0).start())
         self.eight[self.eighth] = self.part[self.rows(self.eighth), :]
 
     def second(self):
         each(1, NODE * CORES, lambda k: self.over_eight(k, 0).wait_recv())
-        for j in range(SIDE):
-            rows = slice(j * STRIP, (j + 1) * STRIP)
-            total = self.eight[0, rows, :]
-            for i in range(1, NODE * CORES):
-                total = total + self.eight[i, rows, :]
-            self.own[j] = total
-        each(1, SIDE, lambda k: self.over_y(k, 1).start())
-        self.along_y[self.y] = self.own[self.y]
+        total = self.eight[0]
+        for i in range(1, NODE * CORES):
+            total = total + self.eight[i]
+        self.along_y[self.y] = total
+        each(1, SIDE, lambda k: self.over_y(k).start())
 
     def third(self):
-        each(1, SIDE, lambda k: self.over_y(k, 1).wait_recv())
+        each(1, SIDE, lambda k: self.over_y(k).wait_recv())
         self.along_z[self.z] = (self.along_y[0] + self.along_y[1]) + (self.along_y[2] + self.along_y[3])
         each(1, SIDE, lambda k: self.over_z(k).start())
 
     def fourth(self):
         each(1, SIDE, lambda k: self.over_z(k).wait_recv())
         total = (self.along_z[0] + self.along_z[1]) + (self.along_z[2] + self.along_z[3])
-        self.total[self.fine(), :] = total
-        each(1, SIDE, lambda k: self.over_y(k, 3).start())
-
-    def fifth(self):
-        each(1, SIDE, lambda k: self.over_y(k, 3).wait_recv())
-        each(1, NODE * CORES, lambda k: self.over_eight(k, 4).start())
+        self.total[self.rows(self.eighth), :] = total
+        each(1, NODE * CORES, lambda k: self.over_eight(k, 3).start())
 
     def last(self):
-        each(1, NODE * CORES, lambda k: self.over_eight(k, 4).wait_recv())
+        each(1, NODE * CORES, lambda k: self.over_eight(k, 3).wait_recv())
         each(1, NODE * CORES, lambda k: self.over_eight(k, 0).wait_send())
-        each(1, SIDE, lambda k: self.over_y(k, 1).wait_send())
+        each(1, SIDE, lambda k: self.over_y(k).wait_send())
         each(1, SIDE, lambda k: self.over_z(k).wait_send())
-        each(1, SIDE, lambda k: self.over_y(k, 3).wait_send())
-        each(1, NODE * CORES, lambda k: self.over_eight(k, 4).wait_send())
+        each(1, NODE * CORES, lambda k: self.over_eight(k, 3).wait_send())
 
 
 def plan_kernel(owner, slot, index, count, req, place, where, seen):
@@ -247,7 +231,7 @@
 def step_kernel(
     item, req, place, where, weights_in, user_in,
     users, user_gram, boxes, table,
-    tiles, full, relay, outbox, inbox_low, inbox_high, asked, lists, weights, user, gram, part, red, mid, eight, own_band, along_y, along_z, high, low, dense,
+    tiles, full, relay, outbox, inbox_low, inbox_high, asked, lists, weights, user, gram, part, red, mid, eight, along_y, along_z, high, low, dense,
     sum_sems, line_sum_sems, row_sems, ask_sems, tile_sems, ring_sems, line_sems, cross_sems, sib_sems,
     load_sems, bring_sems, own_sems, local_sem,
 ):
@@ -517,7 +501,7 @@
 
     pair = split(x)
     part[...] = dot3(pair, pair, (0, 0))
-    summer = LineSummer(part, user_gram, eight, own_band, along_y, along_z, line_sum_sems)
+    summer = LineSummer(part, user_gram, eight, along_y, along_z, line_sum_sems)
     summer.first()
 
     def come_from(way):
@@ -546,8 +530,6 @@
                 sibling(half, along, come_from(way)).start()
         if along == -1:
             summer.fourth()
-        if along == 2:
-            summer.fifth()
     for along in (0, -1, 1, 2):
         for half in range(2):
             for way in range(2):
@@ -612,14 +594,13 @@
             pltpu.VMEM((PLANE, PART, K), F32),
             pltpu.VMEM((NODE * CORES, PART, K), F32),
             pltpu.VMEM((NODE * CORES, BAND, K), F32),
-            pltpu.VMEM((SIDE, STRIP, K), F32),
-            pltpu.VMEM((SIDE, STRIP, K), F32),
-            pltpu.VMEM((SIDE, STRIP, K), F32),
+            pltpu.VMEM((SIDE, BAND, K), F32),
+            pltpu.VMEM((SIDE, BAND, K), F32),
             pltpu.VMEM((PAIRS, K, 2 * TILE), BF16),
             pltpu.VMEM((PAIRS, K, 2 * TILE), BF16),
             pltpu.VMEM((PAIRS, K, 2 * TILE), F32),
             pltpu.SemaphoreType.DMA((3, 2, PLANE)),
-            pltpu.SemaphoreType.DMA((5, 2, NODE * CORES)),
+            pltpu.SemaphoreType.DMA((4, 2, NODE * CORES)),
             pltpu.SemaphoreType.DMA((2, 3, 2)),
             pltpu.SemaphoreType.DMA((2, WIDE)),
             pltpu.SemaphoreType.DMA((2, 2, WIDE)),

time: 132 us -> 132 us (level)
  no operation moved by 1% of the time
where the time goes in v6:
time: 132 us
  Pallas kernels  131 us (99%)
    pallas_call x1, Pallas kernels, step(): pl.pallas_call(step_kernel, out_shape=[pltpu.VMEM((K, K), F32), pltpu.VME...  125 us
    pallas_call x1, Pallas kernels, mask(): pl.pallas_call(mask_kernel, out_shape=[jax.ShapeDtypeStruct((K, K), F32),...  4.38 us

profile of v6, /device:TPU:1, one launch (start us, length us, event | category | flops | bytes accessed | tf_op | source)
XLA Modules:
  0.0 131.9 jit_solution(16253561475613740533)
XLA Ops:
  1.3 1.5 %plan.1 = (s32[128]{0:T(128)}, s32[32]{0:T(128)}, s32[64]{0:T(128)}) custom-call(s32[32]{0:T(128)} %bitcast.5, s32[32]{0:T(128)} %slot.1, s32[64]{0:T(128)} %index.1, s32[1]{0:T(128)S(6)} %copy.10.count), custom_call_target="tpu_custom_call" | custom-call | tf_op jit(solution)/shard_map/plan/pallas_call | solution.py:217
  2.8 124.8 %step.1 = (f32[256,256]{1,0:T(8,128)S(1)}, f32[256,256]{1,0:T(8,128)S(1)}, f32[32,256,256]{2,1,0:T(8,128)S(1)}, s32[32,1,128]{2,1,0:T(1,128)S(1)}) custom-call(f32[64,8192]{1,0:T(8,128)} %bitcast.3, s32[1,128]{1,0:T(1,128)} %bitcast.4, s32[32]{0:T(128)} %get-tuple-element.11.place, s32[64]{0:T(128)} %get-tuple-element.12.where, f32[64,128,128]{2,1,0:T(8,128)} %weights_in.1, ...), custom_call_target="tpu_custom_call" | custom-call | tf_op jit(solution)/shard_map/step/pallas_call | solution.py:571
  127.5 4.4 %mask.1 = (f32[256,256]{1,0:T(8,128)}, f32[256,256]{1,0:T(8,128)}, f32[1,32,256,256]{3,2,1,0:T(8,128)}) custom-call(s32[32,1,128]{2,1,0:T(1,128)S(1)} %get-tuple-element.13.rows, f32[32,256,256]{2,1,0:T(8,128)S(1)} %get-tuple-element.14.boxes, f32[256,256]{1,0:T(8,128)S(1)} %get-tuple-element.15.users_in, f32[256,256]{1,0:T(8,128)S(1)} %get-tuple-element.16.gram_in), custom_call_target="tpu_custom_call" | custom-call | tf_op jit(solution)/shard_map/mask/pallas_call | solution.py:652
